TPU v7x, 128 devices: a whole 4x4x4 slice. The times are simulated.
128 devices in a mesh: wide: 16 (over x, y), narrow: 8 (over z, core).
Axes of the slice: x: 4, y: 4, z: 4, core: 2. Of those that a mesh axis runs over, the one named last changes fastest.
Arguments:
- queries: bfloat16 [16384, 32, 128], P(('wide', 'narrow')), may hold values from -256 to 256
- keys: bfloat16 [16384, 4, 128], P(('wide', 'narrow')), may hold values from -6 to 6
- values: bfloat16 [16384, 4, 128], P(('wide', 'narrow')), may hold values from -6 to 6
- residual: bfloat16 [16384, 4096], P(('wide', 'narrow')), may hold values from -6 to 6
- out_proj: bfloat16 [4096, 4096], P('narrow'), may hold values from -0.09375 to 0.09375
- norm_gain: float32 [4096], replicated, may hold values from 0.25 to 1.75
- expert_ids: int32 [16384, 8], P(('wide', 'narrow')), may hold values from 0 to 127, all different within a row; in each aligned block of 128 rows (0 to 127, 128 to 255, ...) at most 9 rows name the same one
- gate_weights: float32 [16384, 8], P(('wide', 'narrow')), may hold values from 0.03 to 0.3
- w_gate: bfloat16 [128, 4096, 768], P(('wide', 'narrow')), may hold values from -0.09375 to 0.09375
- w_up: bfloat16 [128, 4096, 768], P(('wide', 'narrow')), may hold values from -0.09375 to 0.09375
- w_down: bfloat16 [128, 768, 4096], P(('wide', 'narrow')), may hold values from -0.21875 to 0.21875
Outputs:
- block_out: bfloat16 [16384, 4096], P(('wide', 'narrow'))
Inputs may be any that keep to these rules, and one draw needn't show every extreme that they name: `expert_ids`: in the rows of one device, each expert is named by at most 9 rows; each token names 8 different experts.
All inputs are finite; a program needn't handle non-finite values.
Results may differ from a plain program's by a relative error of at most 0.01.
Values may be sent and summed in bfloat16 or wider, within the bound.
A program may use at most 192 MiB of HBM per device.

v0:
```python
import math

import jax
import jax.numpy as jnp
import numpy as np
from jax import lax
from jax.sharding import PartitionSpec as P


def attend(query_block, key_block, value_block):
    length = query_block.shape[0]
    kv_local = key_block.shape[1]
    per_kv = query_block.shape[1] // kv_local
    head_dim = query_block.shape[2]
    grouped = query_block.reshape(length, kv_local, per_kv, head_dim)
    scores = jnp.einsum(
        "qkgd,skd->kgqs", grouped, key_block, preferred_element_type=jnp.float32
    ) * (1.0 / math.sqrt(head_dim))
    causal = lax.broadcasted_iota(jnp.int32, (length, length), 0) >= lax.broadcasted_iota(
        jnp.int32, (length, length), 1
    )
    scores = jnp.where(causal, scores, -1e30)
    highest = jnp.max(scores, axis=-1, keepdims=True)
    weights = jnp.exp(scores - highest)
    probs = (weights / jnp.sum(weights, axis=-1, keepdims=True)).astype(jnp.bfloat16)
    mixed = jnp.einsum("kgqs,skd->qkgd", probs, value_block, preferred_element_type=jnp.float32)
    return mixed.astype(jnp.bfloat16).reshape(length, kv_local * per_kv * head_dim)


def shards(
    queries,
    keys,
    values,
    residual,
    out_proj,
    norm_gain,
    expert_ids,
    gate_weights,
    w_gate,
    w_up,
    w_down,
):
    narrow_count = lax.axis_size("narrow")
    wide_count = lax.axis_size("wide")
    tok_local = queries.shape[0]
    head_count = queries.shape[1]
    kv_count = keys.shape[1]
    per_device = head_count // narrow_count
    group_size = head_count // kv_count
    kv_local = max(1, per_device // group_size)
    chosen_heads = np.concatenate(
        [
            np.arange(kv_local) + target_dev * per_device // group_size
            for target_dev in range(narrow_count)
        ]
    )
    query_group, key_group, value_group = (
        lax.all_to_all(queries, "narrow", split_axis=1, concat_axis=0, tiled=True),
        lax.all_to_all(keys[:, chosen_heads], "narrow", split_axis=1, concat_axis=0, tiled=True),
        lax.all_to_all(values[:, chosen_heads], "narrow", split_axis=1, concat_axis=0, tiled=True),
    )
    attended = attend(query_group, key_group, value_group)
    projected = lax.psum_scatter(
        jnp.dot(attended, out_proj, preferred_element_type=jnp.float32).astype(jnp.bfloat16),
        "narrow",
        scatter_dimension=0,
        tiled=True,
    ).astype(jnp.float32)
    hidden = residual.astype(jnp.float32) + projected
    normed = (
        hidden * lax.rsqrt(jnp.mean(hidden * hidden, axis=-1, keepdims=True) + 1e-06) * norm_gain
    ).astype(jnp.bfloat16)
    width = normed.shape[1]
    top_count = expert_ids.shape[1]
    local_experts = w_gate.shape[0]
    expert_count = local_experts * wide_count * narrow_count
    device_count = wide_count * narrow_count
    slot_count = (tok_local * top_count * 9 + 8 * expert_count - 1) // (8 * expert_count)
    rows_total = tok_local * top_count
    flat_ids = expert_ids.reshape(rows_total)
    one_hot = (flat_ids[:, None] == jnp.arange(expert_count, dtype=jnp.int32)[None, :]).astype(
        jnp.bfloat16
    )
    lower = (
        lax.broadcasted_iota(jnp.int32, (rows_total, rows_total), 0)
        >= lax.broadcasted_iota(jnp.int32, (rows_total, rows_total), 1)
    ).astype(jnp.bfloat16)
    running = jnp.dot(lower, one_hot, preferred_element_type=jnp.float32)
    rank = (jnp.sum(running * one_hot, axis=1) - 1.0).astype(jnp.int32)
    target = (flat_ids * slot_count + rank).reshape(tok_local, top_count)
    spread_rows = jnp.broadcast_to(normed[:, None, :], (tok_local, top_count, width))
    outgoing = (
        jnp.zeros((expert_count * slot_count, width), jnp.bfloat16).at[target].set(spread_rows)
    )
    arrived_rows = lax.all_to_all(
        outgoing.reshape(device_count, local_experts, slot_count, width),
        ("wide", "narrow"),
        split_axis=0,
        concat_axis=0,
        tiled=True,
    )
    gated = jnp.einsum("sena,eah->senh", arrived_rows, w_gate, preferred_element_type=jnp.float32)
    upward = jnp.einsum("sena,eah->senh", arrived_rows, w_up, preferred_element_type=jnp.float32)
    inner = (jax.nn.silu(gated) * upward).astype(jnp.bfloat16)
    returned = lax.all_to_all(
        jnp.einsum("senh,eha->sena", inner, w_down, preferred_element_type=jnp.float32).astype(
            jnp.bfloat16
        ),
        ("wide", "narrow"),
        split_axis=0,
        concat_axis=0,
        tiled=True,
    )
    returned = returned.reshape(expert_count * slot_count, width)
    mixture = jnp.zeros((tok_local, width), jnp.float32)
    for choice_index in range(top_count):
        mixture = mixture + gate_weights[:, choice_index : choice_index + 1] * returned[
            target[:, choice_index]
        ].astype(jnp.float32)
    return (hidden + mixture).astype(jnp.bfloat16)


def solution(mesh):
    in_specs = (
        P(("wide", "narrow"), None, None),
        P(("wide", "narrow"), None, None),
        P(("wide", "narrow"), None, None),
        P(("wide", "narrow"), None),
        P("narrow", None),
        P(),
        P(("wide", "narrow"), None),
        P(("wide", "narrow"), None),
        P(("wide", "narrow"), None, None),
        P(("wide", "narrow"), None, None),
        P(("wide", "narrow"), None, None),
    )
    out_specs = P(("wide", "narrow"), None)
    return jax.shard_map(shards, mesh=mesh, in_specs=in_specs, out_specs=out_specs, check_vma=False)
```

profile of v0, /device:TPU:50, one launch (start us, length us, event | category | flops | bytes accessed | tf_op | source)
XLA Modules:
  0.0 804.9 jit_solution(2910888163308498303)
XLA Ops:
  9.2 5.4 all-to-all-start.2
  17.3 11.8 %all-to-all-done.2 = bf16[128,32,128]{2,0,1:T(8,128)(2,1)S(1)} async-done(((bf16[128,32,128]{2,0,1:T(8,128)(2,1)}), bf16[128,32,128]{2,0,1:T(8,128)(2,1)S(1)}, u32[]{:S(2)}, u32[]{:S(2)}) %all-to-all-start.2) | async-done | bytes 1048608 | tf_op jit(solution)/shard_map/all_to_all | solution.py:58
  49.3 5.7 copy-done.2
  58.7 9.1 %fusion.26 = bf16[128,4,1024]{2,0,1:T(8,128)(2,1)S(1)} fusion(bf16[1024,128,1]{1,0,2:T(8,128)(2,1)S(1)} %bitcast.148, f32[4,1024]{1,0:T(4,128)S(1)} %fusion, f32[4,1024]{1,0:T(4,128)S(1)} %get-tuple-element.23, f32[1024,1024,4]{1,0,2:T(8,128)} %copy-done.2, pred[1024,1024]{0,1:T(8,128)(4,1)S(1)} %iota_compare_fusion), kind=kOutput, calls=%fused_computation.46 | convolution fusion | flops 1095237632 | bytes 19169280 | tf_op jit(solution)/shard_map/kgqs,skd->qkgd/dot_general | solution.py:26
  67.8 6.9 convolution_convert_fusion
  76.4 49.8 %reduce-scatter.2.cloned.1.call-done = bf16[128,4096]{1,0:T(8,128)(2,1)} async-done(((bf16[1024,4096]{1,0:T(8,128)(2,1)}), bf16[128,4096]{1,0:T(8,128)(2,1)}) %reduce-scatter.2.cloned.1.call-update) | async-done | bytes 1048592 | tf_op jit(solution)/shard_map/reduce_scatter | solution.py:63
  129.5 16.8 %scatter_custom_fusion = bf16[1152,4096]{1,0:T(8,128)(2,1)} fusion(s32[1024]{0:T(1024)S(1)} %reshape.172, bf16[]{:T(256)} %constant.8.clone.1, bf16[128,4096]{1,0:T(8,128)(2,1)S(1)} %multiply_convert_fusion), kind=kCustom, calls=%fused_computation.21 | custom fusion | bytes 10485762 | tf_op jit(solution)/shard_map/scatter | solution.py:93
  146.3 15.1 %reshape.83 = bf16[128,1,9,4096]{3,2,0,1:T(8,128)(2,1)} reshape(bf16[1152,4096]{1,0:T(8,128)(2,1)} %scatter_custom_fusion) | data formatting | bytes 18874368 | tf_op jit(solution)/shard_map/reshape | solution.py:96
  161.4 199.8 %all_to_all.55 = bf16[128,1,9,4096]{3,2,1,0:T(8,128)(2,1)S(1)} all-to-all(bf16[128,1,9,4096]{3,2,1,0:T(8,128)(2,1)} %bitcast.142), channel_id=1, replica_groups=mesh['wide'=16,'narrow'=8] {'wide','narrow'}, dimensions={0} | all-to-all | bytes 18874368 | tf_op jit(solution)/shard_map/all_to_all | solution.py:95
  361.2 39.0 %fusion.2 = f32[128,9,768]{2,0,1:T(8,128)} fusion(bf16[1,4096,768]{2,1,0:T(8,128)(2,1)} %param.23, bf16[128,1,9,4096]{3,2,1,0:T(8,128)(2,1)S(1)} %all_to_all.55), kind=kOutput, calls=%fused_computation.16 | convolution fusion | flops 7247757312 | bytes 19267584 | tf_op jit(solution)/shard_map/sena,eah->senh/dot_general | solution.py:103
  400.2 21.6 %fusion.17 = bf16[128,1,9,768]{3,0,2,1:T(8,128)(2,1)S(1)} fusion(f32[128,9,768]{2,0,1:T(8,128)} %fusion.2, bf16[1,4096,768]{2,1,0:T(8,128)(2,1)} %param.22, bf16[128,1,9,4096]{3,2,1,0:T(8,128)(2,1)S(1)} %all_to_all.55), kind=kOutput, calls=%fused_computation.35 | convolution fusion | flops 7253065728 | bytes 21037056 | tf_op jit(solution)/shard_map/sena,eah->senh/dot_general | solution.py:102
  421.8 10.7 %convert_bitcast_fusion = bf16[128,1,9,4096]{3,0,2,1:T(8,128)(2,1)S(1)} fusion(bf16[1,768,4096]{2,1,0:T(8,128)(2,1)} %param.24, bf16[128,1,9,768]{3,0,2,1:T(8,128)(2,1)S(1)} %fusion.17), kind=kOutput, calls=%fused_computation.20 | convolution fusion | flops 7252475904 | bytes 17498112 | tf_op jit(solution)/shard_map/senh,eha->sena/dot_general | solution.py:106
  432.4 25.0 %copy.60 = bf16[128,1,9,4096]{3,2,1,0:T(8,128)(2,1)} copy(bf16[128,1,9,4096]{3,0,2,1:T(8,128)(2,1)S(1)} %convert_bitcast_fusion) | data formatting | bytes 18874368 | tf_op jit(solution)/shard_map/convert_element_type | solution.py:106
  457.4 13.2 %all-to-all-start.4 = ((bf16[128,1,9,4096]{3,2,1,0:T(8,128)(2,1)}), bf16[128,1,9,4096]{3,2,1,0:T(8,128)(2,1)}, u32[]{:S(2)}, u32[]{:S(2)}) async-start(bf16[128,1,9,4096]{3,2,1,0:T(8,128)(2,1)} %copy.60), calls=%async_computation.5 | async-start | bytes 33554432 | tf_op jit(solution)/shard_map/all_to_all | solution.py:105
  470.8 241.8 %all-to-all-done.4 = bf16[128,1,9,4096]{3,2,1,0:T(8,128)(2,1)} async-done(((bf16[128,1,9,4096]{3,2,1,0:T(8,128)(2,1)}), bf16[128,1,9,4096]{3,2,1,0:T(8,128)(2,1)}, u32[]{:S(2)}, u32[]{:S(2)}) %all-to-all-start.4) | async-done | bytes 9437216 | tf_op jit(solution)/shard_map/all_to_all | solution.py:105
  712.5 16.1 %reshape.89 = bf16[1152,4096]{1,0:T(8,128)(2,1)} reshape(bf16[128,1,9,4096]{3,2,1,0:T(8,128)(2,1)} %all-to-all-done.4) | data formatting | bytes 18874368 | tf_op jit(solution)/shard_map/reshape | solution.py:114
  728.6 7.1 gather_fusion.2
  735.7 8.1 %gather_fusion.3 = bf16[128,4096]{1,0:T(8,128)(2,1)} fusion(bf16[1152,4096]{1,0:T(8,128)(2,1)} %reshape.89, s32[1024]{0:T(1024)S(1)} %get-tuple-element.31), kind=kCustom, calls=%fused_computation.3 | custom fusion | bytes 2097664 | tf_op jit(solution)/shard_map/gather | solution.py:117
  743.8 8.1 %gather_fusion.4 = bf16[128,4096]{1,0:T(8,128)(2,1)} fusion(bf16[1152,4096]{1,0:T(8,128)(2,1)} %reshape.89, s32[1024]{0:T(1024)S(1)} %get-tuple-element.30), kind=kCustom, calls=%fused_computation.4 | custom fusion | bytes 2097664 | tf_op jit(solution)/shard_map/gather | solution.py:117
  751.9 8.3 %gather_fusion.5 = bf16[128,4096]{1,0:T(8,128)(2,1)} fusion(bf16[1152,4096]{1,0:T(8,128)(2,1)} %reshape.89, s32[1024]{0:T(1024)S(1)} %get-tuple-element.29), kind=kCustom, calls=%fused_computation.5 | custom fusion | bytes 2097664 | tf_op jit(solution)/shard_map/gather | solution.py:117
  760.2 8.1 %gather_fusion.6 = bf16[128,4096]{1,0:T(8,128)(2,1)} fusion(bf16[1152,4096]{1,0:T(8,128)(2,1)} %reshape.89, s32[1024]{0:T(1024)S(1)} %get-tuple-element.28), kind=kCustom, calls=%fused_computation.6 | custom fusion | bytes 2097664 | tf_op jit(solution)/shard_map/gather | solution.py:117
  768.3 8.1 %gather_fusion.7 = bf16[128,4096]{1,0:T(8,128)(2,1)} fusion(bf16[1152,4096]{1,0:T(8,128)(2,1)} %reshape.89, s32[1024]{0:T(1024)S(1)} %get-tuple-element.27), kind=kCustom, calls=%fused_computation.7 | custom fusion | bytes 2097664 | tf_op jit(solution)/shard_map/gather | solution.py:117
  776.4 8.1 %gather_fusion.8 = bf16[128,4096]{1,0:T(8,128)(2,1)} fusion(bf16[1152,4096]{1,0:T(8,128)(2,1)} %reshape.89, s32[1024]{0:T(1024)S(1)} %get-tuple-element.26), kind=kCustom, calls=%fused_computation.8 | custom fusion | bytes 2097664 | tf_op jit(solution)/shard_map/gather | solution.py:117
  784.5 8.2 %gather_fusion.9 = bf16[128,4096]{1,0:T(8,128)(2,1)} fusion(bf16[1152,4096]{1,0:T(8,128)(2,1)} %reshape.89, s32[1024]{0:T(1024)S(1)} %get-tuple-element.25), kind=kCustom, calls=%fused_computation.9 | custom fusion | bytes 2097664 | tf_op jit(solution)/shard_map/gather | solution.py:117
  (54 shorter events, 39.4 us)
Async XLA Ops:
  6.5 8.7 %copy-start = (bf16[128,4,128]{2,1,0:T(4,128)(2,1)S(1)}, bf16[128,4,128]{2,1,0:T(4,128)(2,1)}, u32[]{:S(2)}) copy-start(bf16[128,4,128]{2,1,0:T(4,128)(2,1)} %param.15) | copy-start | bytes 393220
  6.5 27.4 %copy-start.3 = (bf16[128,4,128]{2,1,0:T(4,128)(2,1)S(1)}, bf16[128,4,128]{2,1,0:T(4,128)(2,1)}, u32[]{:S(2)}) copy-start(bf16[128,4,128]{2,1,0:T(4,128)(2,1)} %param.16) | copy-start | bytes 393220
  9.2 19.9 %all-to-all-start.2 = ((bf16[128,32,128]{2,0,1:T(8,128)(2,1)}), bf16[128,32,128]{2,0,1:T(8,128)(2,1)S(1)}, u32[]{:S(2)}, u32[]{:S(2)}) async-start(bf16[128,32,128]{2,0,1:T(8,128)(2,1)} %copy.52), calls=%async_computation.2 | async-start | bytes 2097152 | tf_op jit(solution)/shard_map/all_to_all | solution.py:58
  29.1 10.9 %all-to-all-start.1 = ((bf16[128,8,128]{2,0,1:T(8,128)(2,1)}), bf16[128,8,128]{2,0,1:T(8,128)(2,1)S(1)}, u32[]{:S(2)}, u32[]{:S(2)}) async-start(bf16[128,8,128]{2,0,1:T(8,128)(2,1)} %copy.51), calls=%async_computation.1 | async-start | bytes 524288 | tf_op jit(solution)/shard_map/all_to_all | solution.py:59
  40.0 18.7 %all-to-all-start = ((bf16[128,8,128]{2,0,1:T(8,128)(2,1)}), bf16[128,8,128]{2,0,1:T(8,128)(2,1)S(1)}, u32[]{:S(2)}, u32[]{:S(2)}) async-start(bf16[128,8,128]{2,0,1:T(8,128)(2,1)} %copy.49), calls=%async_computation | async-start | bytes 524288 | tf_op jit(solution)/shard_map/all_to_all | solution.py:60
  44.8 81.4 %reduce-scatter.2.cloned.1.call-start = ((), (), s32[]{:S(2)}) async-start(), calls=%async_computation.6 | async-start | bytes 9437184 | tf_op jit(solution)/shard_map/reduce_scatter | solution.py:63
  49.3 5.7 copy-start.2
  58.7 9.1 %copy-start.9 = (bf16[512,4096]{1,0:T(8,128)(2,1)S(1)}, bf16[512,4096]{1,0:T(8,128)(2,1)}, u32[]{:S(2)}) copy-start(bf16[512,4096]{1,0:T(8,128)(2,1)} %param.18) | copy-start | bytes 12582916
  74.6 0.7 copy-start.7
  74.6 51.6 %copy-start.4 = (bf16[128,4096]{1,0:T(8,128)(2,1)S(1)}, bf16[128,4096]{1,0:T(8,128)(2,1)}, u32[]{:S(2)}) copy-start(bf16[128,4096]{1,0:T(8,128)(2,1)} %param.17) | copy-start | bytes 3145732
  74.6 53.2 %copy-start.6 = (f32[4096]{0:T(1024)S(1)}, f32[4096]{0:T(1024)}, u32[]{:S(2)}) copy-start(f32[4096]{0:T(1024)} %param.19) | copy-start | bytes 49156
  457.4 13.3 %copy-start.8 = (f32[128,8]{0,1:T(8,128)S(1)}, f32[128,8]{0,1:T(8,128)}, u32[]{:S(2)}) copy-start(f32[128,8]{0,1:T(8,128)} %param.21) | copy-start | bytes 12292
  457.4 255.1 %all-to-all-start.4 = ((bf16[128,1,9,4096]{3,2,1,0:T(8,128)(2,1)}), bf16[128,1,9,4096]{3,2,1,0:T(8,128)(2,1)}, u32[]{:S(2)}, u32[]{:S(2)}) async-start(bf16[128,1,9,4096]{3,2,1,0:T(8,128)(2,1)} %copy.60), calls=%async_computation.5 | async-start | bytes 33554432 | tf_op jit(solution)/shard_map/all_to_all | solution.py:105
  784.5 8.2 %copy-start.5 = (bf16[128,4096]{1,0:T(8,128)(2,1)S(1)}, bf16[128,4096]{1,0:T(8,128)(2,1)}, u32[]{:S(2)}) copy-start(bf16[128,4096]{1,0:T(8,128)(2,1)} %reduce-scatter.2.cloned.1.call-done) | copy-start | bytes 3145732
  784.5 13.4 %copy-start.1 = (bf16[128,4,128]{2,1,0:T(4,128)(2,1)S(1)}, bf16[128,4,128]{2,1,0:T(4,128)(2,1)}, u32[]{:S(2)}) copy-start(bf16[128,4,128]{2,1,0:T(4,128)(2,1)} %param.15) | copy-start | bytes 393220
Sparse Core Ops, SparseCore 0:
  74.8 51.3 reduce-scatter.1
where the time goes:
time: 809 us; the launch traced here: 805 us
  waiting for transfers between devices  307 us (38%)
  blocking collectives  200 us (25%)
  local copies, waits for them, and re-layouts  151 us (19%)
  matrix products  91.6 us (11%)
  starting transfers between devices  28.7 us (4%)
  between operations  13.8 us (2%)
  other arithmetic  13.2 us (2%)
    all_to_all x1, waiting for transfers between devices, shards(): lax.all_to_all(jnp.einsum('senh,eha->sena', inner, w_down, preferred_elem...  242 us
    all_to_all x1, blocking collectives, shards(): lax.all_to_all(outgoing.reshape(device_count, local_experts, slot_count,...  200 us
    gather x8, local copies, waits for them, and re-layouts, shards(): returned[target[:, choice_index]].astype(jnp.float32)  64 us
    reduce_scatter x1, waiting for transfers between devices, shards(): lax.psum_scatter(jnp.dot(attended, out_proj, preferred_element_type=jnp.f...  49.8 us
    dot_general x1, matrix products, shards(): jnp.einsum('sena,eah->senh', arrived_rows, w_up, preferred_element_type=j...  39 us
    convert_element_type x1, local copies, waits for them, and re-layouts, shards(): jnp.einsum('senh,eha->sena', inner, w_down, preferred_element_type=jnp.fl...  25 us
    dot_general x1, matrix products, shards(): jnp.einsum('sena,eah->senh', arrived_rows, w_gate, preferred_element_type...  21.6 us
    scatter x1, local copies, waits for them, and re-layouts, shards(): jnp.zeros((expert_count * slot_count, width), jnp.bfloat16).at[target]  16.8 us
  transfers between devices with their start and end apart: 5, of which 4 were waited for; matrix products, arithmetic and copies ran while one was open for 2% of the time, Pallas kernels for 0%

commit v1 on v0

v1 whole, which is shorter than its diff:
```python
import math

import jax
import jax.numpy as jnp
import numpy as np
from jax import lax
from jax.experimental import pallas as pl
from jax.experimental.pallas import tpu as pltpu
from jax.sharding import PartitionSpec as P

MESH = pl.DeviceIdType.MESH
BF = jnp.bfloat16
F32 = jnp.float32


def offset_of(k):
    return k % 4, (k // 4 + k) % 4, (k // 16 + k // 4 + k) % 4, k // 64


def peer_of(k, sign):
    wide, narrow = lax.axis_index("wide"), lax.axis_index("narrow")
    dx, dy, dz, dc = offset_of(k)
    x = (wide // 4 + sign * dx + 4) % 4
    y = (wide % 4 + sign * dy + 4) % 4
    z = (narrow // 2 + sign * dz + 4) % 4
    c = (narrow % 2 + dc) % 2
    return (x * 4 + y, z * 2 + c)


def iota2(shape, dim):
    return lax.broadcasted_iota(jnp.int32, shape, dim)


def moe_kernel(
    normed,
    hidden,
    pick,
    pick8,
    mix_hi,
    mix_lo,
    mix8_hi,
    mix8_lo,
    wg_hbm,
    wu_hbm,
    wd_hbm,
    out,
    stage,
    recv,
    ret,
    wg,
    wu,
    wd,
    n2,
    g8,
    rows,
    inner,
    acc,
    w_sem,
    d_send,
    d_recv,
    r_send,
    r_recv,
):
    barrier = pltpu.get_barrier_semaphore()

    @pl.loop(1, 128)
    def _(k):
        pl.semaphore_signal(barrier, inc=1, device_id=peer_of(k, 1), device_id_type=MESH)

    loads = [
        pltpu.make_async_copy(src.at[0], dst, w_sem.at[i])
        for i, (src, dst) in enumerate(((wg_hbm, wg), (wu_hbm, wu), (wd_hbm, wd)))
    ]
    for load in loads:
        load.start()

    to_row = iota2((256, 256), 0)
    to_col = iota2((256, 256), 1)

    def folded(i):
        return ((i >> 3) & 15) * 16 + (i >> 7) * 8 + (i & 7)

    unfold = (to_col == folded(to_row)).astype(F32).astype(BF)
    fold = (to_row == folded(to_col)).astype(F32).astype(BF)
    swap = (to_col == (to_row & 15) * 16 + (to_row >> 4)).astype(F32).astype(BF)

    def dot(a, b):
        return jnp.dot(a, b, preferred_element_type=F32)

    def slab(k):
        return pl.ds(pl.multiple_of(k * 16, 16), 16)

    def group(q):
        return pl.ds(pl.multiple_of(q * 256, 256), 256)

    def dispatch(k):
        return pltpu.make_async_remote_copy(
            src_ref=stage.at[slab(k)],
            dst_ref=recv.at[slab(k)],
            send_sem=d_send.at[k],
            recv_sem=d_recv.at[k],
            device_id=peer_of(k, 1),
            device_id_type=MESH,
        )

    def give_back(k):
        return pltpu.make_async_remote_copy(
            src_ref=recv.at[slab(k)],
            dst_ref=ret.at[slab(k)],
            send_sem=r_send.at[k],
            recv_sem=r_recv.at[k],
            device_id=peer_of(k, -1),
            device_id_type=MESH,
        )

    own_in = pltpu.make_async_copy(stage.at[pl.ds(0, 16)], recv.at[pl.ds(0, 16)], d_recv.at[0])
    own_out = pltpu.make_async_copy(recv.at[pl.ds(0, 16)], ret.at[pl.ds(0, 16)], r_recv.at[0])

    n2[0:128, :] = normed[:, 0:2048]
    n2[128:256, :] = normed[:, 2048:4096]

    @pl.loop(0, 4)
    def _(n):
        cols = pl.ds(pl.multiple_of(n * 1024, 1024), 1024)
        g8[:, cols] = dot(pick8[...], normed[:, cols]).astype(BF)

    pl.semaphore_wait(barrier, 127)

    @pl.loop(0, 8)
    def _(q):
        for n in range(4):
            stage[group(q), n * 512 : (n + 1) * 512] = dot(
                pick[group(q), :], n2[:, n * 512 : (n + 1) * 512]
            ).astype(BF)
        some = g8[slab(q), :]
        piled = jnp.concatenate([some[:, g * 256 : (g + 1) * 256] for g in range(16)], axis=0)
        stage[group(q), 2048:2304] = dot(swap, piled).astype(BF)

        @pl.loop(0, 16)
        def _(i):
            k = q * 16 + i

            @pl.when(k > 0)
            def _():
                dispatch(k).start()

    own_in.start()
    for load in loads:
        load.wait()

    @pl.loop(0, 4)
    def _(j):
        @pl.loop(0, 32)
        def _(i):
            k = j * 32 + i

            @pl.when(k > 0)
            def _():
                dispatch(k).wait_recv()

            @pl.when(k == 0)
            def _():
                own_in.wait()

        for q in range(2):
            part = group(j * 2 + q)
            for n in range(4):
                cols = slice(n * 512, (n + 1) * 512)
                wide_rows = dot(unfold, recv[part, cols]).astype(BF)
                rows[q * 128 : (q + 1) * 128, n * 512 : (n + 1) * 512] = wide_rows[0:128]
                rows[q * 128 : (q + 1) * 128, 2048 + n * 512 : 2048 + (n + 1) * 512] = wide_rows[
                    128:256
                ]
            last = dot(swap, recv[part, 2048:2304]).astype(BF)
            for g in range(16):
                rows[256 + q * 16 : 272 + q * 16, g * 256 : (g + 1) * 256] = last[
                    g * 16 : (g + 1) * 16
                ]

        @pl.loop(0, 3)
        def _(n):
            cols = pl.ds(pl.multiple_of(n * 256, 256), 256)
            gated = dot(rows[...], wg[:, cols])
            upward = dot(rows[...], wu[:, cols])
            inner[:, cols] = (gated / (1.0 + jnp.exp(-gated)) * upward).astype(BF)

        @pl.loop(0, 8)
        def _(n):
            cols = pl.ds(pl.multiple_of(n * 512, 512), 512)
            rows[:, cols] = dot(inner[...], wd[:, cols]).astype(BF)

        for q in range(2):
            part = group(j * 2 + q)
            for n in range(4):
                piled = jnp.concatenate(
                    [
                        rows[q * 128 : (q + 1) * 128, n * 512 : (n + 1) * 512],
                        rows[q * 128 : (q + 1) * 128, 2048 + n * 512 : 2048 + (n + 1) * 512],
                    ],
                    axis=0,
                )
                recv[part, n * 512 : (n + 1) * 512] = dot(fold, piled).astype(BF)
            piled = jnp.concatenate(
                [
                    rows[256 + q * 16 : 272 + q * 16, g * 256 : (g + 1) * 256]
                    for g in range(16)
                ],
                axis=0,
            )
            recv[part, 2048:2304] = dot(swap, piled).astype(BF)

        @pl.loop(0, 32)
        def _(i):
            k = j * 32 + i

            @pl.when(k > 0)
            def _():
                give_back(k).start()

            @pl.when(k == 0)
            def _():
                own_out.start()

    acc[...] = jnp.zeros_like(acc)

    @pl.loop(0, 8)
    def _(q):
        @pl.loop(0, 16)
        def _(i):
            k = q * 16 + i

            @pl.when(k > 0)
            def _():
                give_back(k).wait_recv()

            @pl.when(k == 0)
            def _():
                own_out.wait()

        span = pl.ds(pl.multiple_of(q * 256, 256), 256)
        for n in range(4):
            cols = slice(n * 512, (n + 1) * 512)
            block = ret[group(q), cols]
            acc[:, cols] += dot(mix_hi[:, span], block) + dot(mix_lo[:, span], block)
        last = dot(swap, ret[group(q), 2048:2304]).astype(BF)
        for g in range(16):
            g8[slab(q), g * 256 : (g + 1) * 256] = last[g * 16 : (g + 1) * 16]

    for n in range(8):
        cols = slice(n * 512, (n + 1) * 512)
        half, inside = n // 4, slice((n % 4) * 512, (n % 4 + 1) * 512)
        block = g8[:, cols]
        total = acc[half * 128 : (half + 1) * 128, inside]
        total = total + dot(mix8_hi[...], block) + dot(mix8_lo[...], block)
        out[:, cols] = (hidden[:, cols] + total).astype(BF)

    @pl.loop(1, 128)
    def _(k):
        dispatch(k).wait_send()
        give_back(k).wait_send()


def moe(normed, hidden, expert_ids, gate_weights, w_gate, w_up, w_down):
    steps = jnp.arange(128, dtype=jnp.int32)
    wide, narrow = peer_of(steps, 1)
    expert_at = wide * 8 + narrow
    named = expert_ids[:, :, None] == expert_at[None, None, :]
    chosen = jnp.any(named, axis=1)
    weight = jnp.sum(jnp.where(named, gate_weights[:, :, None], 0.0), axis=1)
    before = iota2((128, 128), 0) > iota2((128, 128), 1)
    rank = jnp.dot(before.astype(BF), chosen.astype(BF), preferred_element_type=F32)
    rank = jnp.where(chosen, rank.astype(jnp.int32), -1)
    slots = jnp.arange(8, dtype=jnp.int32)
    at_slot = rank[:, :, None] == slots[None, None, :]
    mix = jnp.where(at_slot, weight[:, :, None], 0.0)

    def both_halves(a):
        zero = jnp.zeros_like(a)
        top = jnp.stack([a, zero], axis=2).reshape(128, 2048)
        low = jnp.stack([zero, a], axis=2).reshape(128, 2048)
        return jnp.concatenate([top, low], axis=0)

    pick = both_halves(at_slot.astype(BF)).T
    mix_hi = both_halves(mix).astype(BF)
    mix_lo = both_halves(mix - mix.astype(BF).astype(F32)).astype(BF)
    at_last = rank == 8
    pick8 = at_last.astype(BF).T
    mix8 = jnp.where(at_last, weight, 0.0)
    mix8_hi = mix8.astype(BF)
    mix8_lo = (mix8 - mix8_hi.astype(F32)).astype(BF)

    vmem = pl.BlockSpec(memory_space=pltpu.VMEM)
    hbm = pl.BlockSpec(memory_space=pl.ANY)
    return pl.pallas_call(
        moe_kernel,
        out_shape=jax.ShapeDtypeStruct((128, 4096), BF),
        in_specs=[vmem] * 8 + [hbm] * 3,
        out_specs=vmem,
        scratch_shapes=[
            pltpu.VMEM((2048, 2304), BF),
            pltpu.VMEM((2048, 2304), BF),
            pltpu.VMEM((2048, 2304), BF),
            pltpu.VMEM((4096, 768), BF),
            pltpu.VMEM((4096, 768), BF),
            pltpu.VMEM((768, 4096), BF),
            pltpu.VMEM((256, 2048), BF),
            pltpu.VMEM((128, 4096), BF),
            pltpu.VMEM((288, 4096), BF),
            pltpu.VMEM((288, 768), BF),
            pltpu.VMEM((256, 2048), F32),
            pltpu.SemaphoreType.DMA((3,)),
            pltpu.SemaphoreType.DMA((128,)),
            pltpu.SemaphoreType.DMA((128,)),
            pltpu.SemaphoreType.DMA((128,)),
            pltpu.SemaphoreType.DMA((128,)),
        ],
        compiler_params=pltpu.CompilerParams(
            collective_id=1, has_side_effects=True, vmem_limit_bytes=63 * 2**20
        ),
        cost_estimate=pl.CostEstimate(
            flops=25_000_000_000, bytes_accessed=25_000_000, transcendentals=1_000_000
        ),
    )(normed, hidden, pick, pick8, mix_hi, mix_lo, mix8_hi, mix8_lo, w_gate, w_up, w_down)


def attend(query_block, key_block, value_block):
    length = query_block.shape[0]
    kv_local = key_block.shape[1]
    per_kv = query_block.shape[1] // kv_local
    head_dim = query_block.shape[2]
    grouped = query_block.reshape(length, kv_local, per_kv, head_dim)
    scores = jnp.einsum(
        "qkgd,skd->kgqs", grouped, key_block, preferred_element_type=jnp.float32
    ) * (1.0 / math.sqrt(head_dim))
    causal = lax.broadcasted_iota(jnp.int32, (length, length), 0) >= lax.broadcasted_iota(
        jnp.int32, (length, length), 1
    )
    scores = jnp.where(causal, scores, -1e30)
    highest = jnp.max(scores, axis=-1, keepdims=True)
    weights = jnp.exp(scores - highest)
    probs = (weights / jnp.sum(weights, axis=-1, keepdims=True)).astype(jnp.bfloat16)
    mixed = jnp.einsum("kgqs,skd->qkgd", probs, value_block, preferred_element_type=jnp.float32)
    return mixed.astype(jnp.bfloat16).reshape(length, kv_local * per_kv * head_dim)


def shards(
    queries,
    keys,
    values,
    residual,
    out_proj,
    norm_gain,
    expert_ids,
    gate_weights,
    w_gate,
    w_up,
    w_down,
):
    narrow_count = lax.axis_size("narrow")
    head_count = queries.shape[1]
    kv_count = keys.shape[1]
    per_device = head_count // narrow_count
    group_size = head_count // kv_count
    kv_local = max(1, per_device // group_size)
    chosen_heads = np.concatenate(
        [
            np.arange(kv_local) + target_dev * per_device // group_size
            for target_dev in range(narrow_count)
        ]
    )
    query_group, key_group, value_group = (
        lax.all_to_all(queries, "narrow", split_axis=1, concat_axis=0, tiled=True),
        lax.all_to_all(keys[:, chosen_heads], "narrow", split_axis=1, concat_axis=0, tiled=True),
        lax.all_to_all(values[:, chosen_heads], "narrow", split_axis=1, concat_axis=0, tiled=True),
    )
    attended = attend(query_group, key_group, value_group)
    projected = lax.psum_scatter(
        jnp.dot(attended, out_proj, preferred_element_type=jnp.float32).astype(jnp.bfloat16),
        "narrow",
        scatter_dimension=0,
        tiled=True,
    ).astype(jnp.float32)
    hidden = residual.astype(jnp.float32) + projected
    normed = (
        hidden * lax.rsqrt(jnp.mean(hidden * hidden, axis=-1, keepdims=True) + 1e-06) * norm_gain
    ).astype(jnp.bfloat16)
    return moe(normed, hidden, expert_ids, gate_weights, w_gate, w_up, w_down)


def solution(mesh):
    in_specs = (
        P(("wide", "narrow"), None, None),
        P(("wide", "narrow"), None, None),
        P(("wide", "narrow"), None, None),
        P(("wide", "narrow"), None),
        P("narrow", None),
        P(),
        P(("wide", "narrow"), None),
        P(("wide", "narrow"), None),
        P(("wide", "narrow"), None, None),
        P(("wide", "narrow"), None, None),
        P(("wide", "narrow"), None, None),
    )
    out_specs = P(("wide", "narrow"), None)
    return jax.shard_map(shards, mesh=mesh, in_specs=in_specs, out_specs=out_specs, check_vma=False)
```

time: 809 us -> 416 us (0.51)
  the two profiles are of different devices: /device:TPU:50 before, /device:TPU:1 now
where the time goes in v1:
time: 416 us
  Pallas kernels  272 us (65%)
  waiting for transfers between devices  57.9 us (14%)
  local copies, waits for them, and re-layouts  21.1 us (5%)
  matrix products  20.6 us (5%)
  starting transfers between devices  15.4 us (4%)
  other arithmetic  14.8 us (4%)
  between operations  13.7 us (3%)
    pallas_call x1, Pallas kernels, moe(): pl.pallas_call(moe_kernel, out_shape=jax.ShapeDtypeStruct((128, 4096), BF...  272 us
    reduce_scatter x1, waiting for transfers between devices, shards(): lax.psum_scatter(jnp.dot(attended, out_proj, preferred_element_type=jnp.f...  41.5 us
    all_to_all x1, waiting for transfers between devices, shards(): lax.all_to_all(queries, 'narrow', split_axis=1, concat_axis=0, tiled=True)  12.4 us
    unnamed x30, local copies, waits for them, and re-layouts  11.5 us
    dot_general x1, matrix products, attend(): jnp.einsum('kgqs,skd->qkgd', probs, value_block, preferred_element_type=j...  9.07 us
  transfers between devices with their start and end apart: 4, of which 3 were waited for; matrix products, arithmetic and copies ran while one was open for 6% of the time, Pallas kernels for 0%

profile of v1, /device:TPU:1, one launch (start us, length us, event | category | flops | bytes accessed | tf_op | source)
XLA Modules:
  0.0 415.6 jit_solution(5250414681560314535)
XLA Ops:
  6.5 2.6 copy.55
  9.2 6.8 %all-to-all-start.2 = ((bf16[128,32,128]{2,0,1:T(8,128)(2,1)}), bf16[128,32,128]{2,0,1:T(8,128)(2,1)S(1)}, u32[]{:S(2)}, u32[]{:S(2)}) async-start(bf16[128,32,128]{2,0,1:T(8,128)(2,1)} %copy.55), calls=%async_computation.2 | async-start | bytes 2097152 | tf_op jit(solution)/shard_map/all_to_all | solution.py:372
  16.7 1.3 gather_fusion.1
  18.7 12.4 %all-to-all-done.2 = bf16[128,32,128]{2,0,1:T(8,128)(2,1)S(1)} async-done(((bf16[128,32,128]{2,0,1:T(8,128)(2,1)}), bf16[128,32,128]{2,0,1:T(8,128)(2,1)S(1)}, u32[]{:S(2)}, u32[]{:S(2)}) %all-to-all-start.2) | async-done | bytes 1048608 | tf_op jit(solution)/shard_map/all_to_all | solution.py:372
  31.1 4.2 %all-to-all-start.1 = ((bf16[128,8,128]{2,0,1:T(8,128)(2,1)}), bf16[128,8,128]{2,0,1:T(8,128)(2,1)S(1)}, u32[]{:S(2)}, u32[]{:S(2)}) async-start(bf16[128,8,128]{2,0,1:T(8,128)(2,1)} %copy.54), calls=%async_computation.1 | async-start | bytes 524288 | tf_op jit(solution)/shard_map/all_to_all | solution.py:373
  35.3 1.3 gather_fusion
  37.8 4.0 all-to-all-done.1
  41.8 4.4 %all-to-all-start = ((bf16[128,8,128]{2,0,1:T(8,128)(2,1)}), bf16[128,8,128]{2,0,1:T(8,128)(2,1)S(1)}, u32[]{:S(2)}, u32[]{:S(2)}) async-start(bf16[128,8,128]{2,0,1:T(8,128)(2,1)} %copy.52), calls=%async_computation | async-start | bytes 524288 | tf_op jit(solution)/shard_map/all_to_all | solution.py:374
  46.2 4.0 fusion.1
  50.2 5.7 %copy-done.2 = f32[1024,1024,4]{1,0,2:T(8,128)} copy-done((f32[1024,1024,4]{1,0,2:T(8,128)}, f32[1024,1024,4]{1,0,2:T(8,128)S(1)}, u32[]{:S(2)}) %copy-start.2) | copy-done | bytes 16777240
  55.9 3.7 fusion
  59.6 9.1 %fusion.4 = bf16[128,4,1024]{2,0,1:T(8,128)(2,1)S(1)} fusion(bf16[1024,128,1]{1,0,2:T(8,128)(2,1)S(1)} %bitcast.73, f32[4,1024]{1,0:T(4,128)S(1)} %fusion, f32[4,1024]{1,0:T(4,128)S(1)} %get-tuple-element.15, f32[1024,1024,4]{1,0,2:T(8,128)} %copy-done.2, pred[1024,1024]{0,1:T(8,128)(4,1)S(1)} %iota_compare_fusion), kind=kOutput, calls=%fused_computation.14 | convolution fusion | flops 1095237632 | bytes 19169280 | tf_op jit(solution)/shard_map/kgqs,skd->qkgd/dot_general | solution.py:342
  68.7 6.8 %convolution_convert_fusion = bf16[1024,4096]{1,0:T(8,128)(2,1)} fusion(bf16[1024,512]{0,1:T(8,128)(2,1)S(1)} %bitcast.74, bf16[512,4096]{1,0:T(8,128)(2,1)S(1)} %copy-done.12), kind=kOutput, calls=%fused_computation.9 | convolution fusion | flops 4299161600 | bytes 13631488 | tf_op jit(solution)/shard_map/dot_general | solution.py:378
  79.2 1.0 copy.63
  80.2 1.0 copy.62
  82.3 1.0 copy.64
  84.1 1.1 maximum_bitcast_fusion.pick
  85.2 1.0 pad_maximum_fusion.mix_hi
  86.2 1.1 pad_maximum_fusion.1.mix_lo
  87.3 41.5 %reduce-scatter.2.cloned.1.call-done = bf16[128,4096]{1,0:T(8,128)(2,1)} async-done(((bf16[1024,4096]{1,0:T(8,128)(2,1)}), bf16[128,4096]{1,0:T(8,128)(2,1)}) %reduce-scatter.2.cloned.1.call-update) | async-done | bytes 1048592 | tf_op jit(solution)/shard_map/reduce_scatter | solution.py:377
  128.8 2.9 convert_add_fusion
  131.7 2.6 multiply_convert_fusion.normed
  134.3 272.1 %shard_map.136 = bf16[128,4096]{1,0:T(8,128)(2,1)} custom-call(bf16[128,4096]{1,0:T(8,128)(2,1)} %multiply_convert_fusion.normed, f32[128,4096]{1,0:T(8,128)} %get-tuple-element.7.hidden, bf16[2048,256]{1,0:T(8,128)(2,1)} %maximum_bitcast_fusion.pick, bf16[128,128]{1,0:T(8,128)(2,1)} %copy.66.pick8, bf16[256,2048]{1,0:T(8,128)(2,1)} %pad_maximum_fusion.mix_hi, ...), custom_call_target="tpu_custom_call" | custom-call | flops 24999999488 | bytes 25000000 | tf_op jit(solution)/shard_map/pallas_call | solution.py:294
  406.5 2.3 copy.70
  (51 shorter events, 8.0 us)
Async XLA Ops:
  6.5 10.1 %copy-start = (bf16[128,4,128]{2,1,0:T(4,128)(2,1)S(1)}, bf16[128,4,128]{2,1,0:T(4,128)(2,1)}, u32[]{:S(2)}) copy-start(bf16[128,4,128]{2,1,0:T(4,128)(2,1)} %param.15) | copy-start | bytes 393220
  6.5 28.7 %copy-start.3 = (bf16[128,4,128]{2,1,0:T(4,128)(2,1)S(1)}, bf16[128,4,128]{2,1,0:T(4,128)(2,1)}, u32[]{:S(2)}) copy-start(bf16[128,4,128]{2,1,0:T(4,128)(2,1)} %param.16) | copy-start | bytes 393220
  9.2 21.9 %all-to-all-start.2 = ((bf16[128,32,128]{2,0,1:T(8,128)(2,1)}), bf16[128,32,128]{2,0,1:T(8,128)(2,1)S(1)}, u32[]{:S(2)}, u32[]{:S(2)}) async-start(bf16[128,32,128]{2,0,1:T(8,128)(2,1)} %copy.55), calls=%async_computation.2 | async-start | bytes 2097152 | tf_op jit(solution)/shard_map/all_to_all | solution.py:372
  31.1 10.7 %all-to-all-start.1 = ((bf16[128,8,128]{2,0,1:T(8,128)(2,1)}), bf16[128,8,128]{2,0,1:T(8,128)(2,1)S(1)}, u32[]{:S(2)}, u32[]{:S(2)}) async-start(bf16[128,8,128]{2,0,1:T(8,128)(2,1)} %copy.54), calls=%async_computation.1 | async-start | bytes 524288 | tf_op jit(solution)/shard_map/all_to_all | solution.py:373
  41.8 17.8 %all-to-all-start = ((bf16[128,8,128]{2,0,1:T(8,128)(2,1)}), bf16[128,8,128]{2,0,1:T(8,128)(2,1)S(1)}, u32[]{:S(2)}, u32[]{:S(2)}) async-start(bf16[128,8,128]{2,0,1:T(8,128)(2,1)} %copy.52), calls=%async_computation | async-start | bytes 524288 | tf_op jit(solution)/shard_map/all_to_all | solution.py:374
  46.2 82.7 %reduce-scatter.2.cloned.1.call-start = ((), (), s32[]{:S(2)}) async-start(), calls=%async_computation.4 | async-start | bytes 9437184 | tf_op jit(solution)/shard_map/reduce_scatter | solution.py:377
  50.2 5.7 %copy-start.2 = (f32[1024,1024,4]{1,0,2:T(8,128)}, f32[1024,1024,4]{1,0,2:T(8,128)S(1)}, u32[]{:S(2)}) copy-start(f32[1024,1024,4]{1,0,2:T(8,128)S(1)} %get-tuple-element.16) | copy-start | bytes 50331652
  59.6 9.1 %copy-start.12 = (bf16[512,4096]{1,0:T(8,128)(2,1)S(1)}, bf16[512,4096]{1,0:T(8,128)(2,1)}, u32[]{:S(2)}) copy-start(bf16[512,4096]{1,0:T(8,128)(2,1)} %param.18) | copy-start | bytes 12582916
  75.5 0.7 copy-start.10
  75.5 0.8 copy-start.11
  79.2 49.6 %copy-start.4 = (bf16[128,4096]{1,0:T(8,128)(2,1)S(1)}, bf16[128,4096]{1,0:T(8,128)(2,1)}, u32[]{:S(2)}) copy-start(bf16[128,4096]{1,0:T(8,128)(2,1)} %param.17) | copy-start | bytes 3145732
  80.2 5.0 %copy-start.5 = (bf16[128,2048]{1,0:T(8,128)(2,1)S(1)}, bf16[128,2048]{1,0:T(8,128)(2,1)}, u32[]{:S(2)}) copy-start(bf16[128,2048]{1,0:T(8,128)(2,1)} %copy.63) | copy-start | bytes 1572868
  81.3 3.9 copy-start.6
  82.3 4.0 copy-start.7
  83.3 3.0 copy-start.8
  83.3 48.5 %copy-start.9 = (f32[4096]{0:T(1024)S(1)}, f32[4096]{0:T(1024)}, u32[]{:S(2)}) copy-start(f32[4096]{0:T(1024)} %param.19) | copy-start | bytes 49156
  134.3 274.4 %copy-start.1 = (bf16[128,4,128]{2,1,0:T(4,128)(2,1)S(1)}, bf16[128,4,128]{2,1,0:T(4,128)(2,1)}, u32[]{:S(2)}) copy-start(bf16[128,4,128]{2,1,0:T(4,128)(2,1)} %param.15) | copy-start | bytes 393220
Sparse Core Ops, SparseCore 0:
  75.6 53.1 reduce-scatter.1

commit v2 on v1

--- a/solution.py
+++ b/solution.py
@@ -2,7 +2,6 @@
 
 import jax
 import jax.numpy as jnp
-import numpy as np
 from jax import lax
 from jax.experimental import pallas as pl
 from jax.experimental.pallas import tpu as pltpu
@@ -31,15 +30,17 @@
     return lax.broadcasted_iota(jnp.int32, shape, dim)
 
 
+def dot(a, b):
+    return jnp.dot(a, b, preferred_element_type=F32)
+
+
 def moe_kernel(
     normed,
     hidden,
-    pick,
-    pick8,
-    mix_hi,
-    mix_lo,
-    mix8_hi,
-    mix8_lo,
+    rank,
+    rank_t,
+    share_hi,
+    share_lo,
     wg_hbm,
     wu_hbm,
     wd_hbm,
@@ -80,12 +81,12 @@
     def folded(i):
         return ((i >> 3) & 15) * 16 + (i >> 7) * 8 + (i & 7)
 
-    unfold = (to_col == folded(to_row)).astype(F32).astype(BF)
-    fold = (to_row == folded(to_col)).astype(F32).astype(BF)
-    swap = (to_col == (to_row & 15) * 16 + (to_row >> 4)).astype(F32).astype(BF)
-
-    def dot(a, b):
-        return jnp.dot(a, b, preferred_element_type=F32)
+    def ones_where(mask):
+        return jnp.where(mask, 1.0, 0.0).astype(BF)
+
+    unfold = ones_where(to_col == folded(to_row))
+    fold = ones_where(to_row == folded(to_col))
+    swap = ones_where(to_col == (to_row & 15) * 16 + (to_row >> 4))
 
     def slab(k):
         return pl.ds(pl.multiple_of(k * 16, 16), 16)
@@ -118,19 +119,29 @@
 
     n2[0:128, :] = normed[:, 0:2048]
     n2[128:256, :] = normed[:, 2048:4096]
+    pick8 = ones_where(rank_t[...] == 8.0)
 
     @pl.loop(0, 4)
     def _(n):
         cols = pl.ds(pl.multiple_of(n * 1024, 1024), 1024)
-        g8[:, cols] = dot(pick8[...], normed[:, cols]).astype(BF)
+        g8[:, cols] = dot(pick8, normed[:, cols]).astype(BF)
+
+    spread_row, spread_col = iota2((256, 128), 0), iota2((256, 128), 1)
+    slot_row = (spread_row & 7).astype(F32)
+    low_row = (spread_row & 8) == 0
 
     pl.semaphore_wait(barrier, 127)
 
     @pl.loop(0, 8)
     def _(q):
+        spread = ones_where((spread_row >> 4) + q * 16 == spread_col)
+        hit = dot(spread, rank_t[...].astype(BF)) == slot_row
+        pick = jnp.concatenate(
+            [ones_where(hit & low_row), ones_where(hit & jnp.logical_not(low_row))], axis=1
+        )
         for n in range(4):
             stage[group(q), n * 512 : (n + 1) * 512] = dot(
-                pick[group(q), :], n2[:, n * 512 : (n + 1) * 512]
+                pick, n2[:, n * 512 : (n + 1) * 512]
             ).astype(BF)
         some = g8[slab(q), :]
         piled = jnp.concatenate([some[:, g * 256 : (g + 1) * 256] for g in range(16)], axis=0)
@@ -222,6 +233,9 @@
                 own_out.start()
 
     acc[...] = jnp.zeros_like(acc)
+    lane_row, lane_col = iota2((128, 256), 0), iota2((128, 256), 1)
+    slot_col = (lane_col & 7).astype(F32)
+    low_col = (lane_col & 8) == 0
 
     @pl.loop(0, 8)
     def _(q):
@@ -237,21 +251,34 @@
             def _():
                 own_out.wait()
 
-        span = pl.ds(pl.multiple_of(q * 256, 256), 256)
+        spread = ones_where((lane_col >> 4) + q * 16 == lane_row)
+        hit = dot(rank[...].astype(BF), spread) == slot_col
+        high = jnp.where(hit, dot(share_hi[...], spread), 0.0)
+        low = jnp.where(hit, dot(share_lo[...], spread), 0.0)
+
+        def both(a):
+            return jnp.concatenate(
+                [jnp.where(low_col, a, 0.0), jnp.where(low_col, 0.0, a)], axis=0
+            ).astype(BF)
+
+        mix_hi, mix_lo = both(high), both(low)
         for n in range(4):
             cols = slice(n * 512, (n + 1) * 512)
             block = ret[group(q), cols]
-            acc[:, cols] += dot(mix_hi[:, span], block) + dot(mix_lo[:, span], block)
+            acc[:, cols] += dot(mix_hi, block) + dot(mix_lo, block)
         last = dot(swap, ret[group(q), 2048:2304]).astype(BF)
         for g in range(16):
             g8[slab(q), g * 256 : (g + 1) * 256] = last[g * 16 : (g + 1) * 16]
 
+    at_last = rank[...] == 8.0
+    mix8_hi = jnp.where(at_last, share_hi[...].astype(F32), 0.0).astype(BF)
+    mix8_lo = jnp.where(at_last, share_lo[...].astype(F32), 0.0).astype(BF)
     for n in range(8):
         cols = slice(n * 512, (n + 1) * 512)
         half, inside = n // 4, slice((n % 4) * 512, (n % 4 + 1) * 512)
         block = g8[:, cols]
         total = acc[half * 128 : (half + 1) * 128, inside]
-        total = total + dot(mix8_hi[...], block) + dot(mix8_lo[...], block)
+        total = total + dot(mix8_hi, block) + dot(mix8_lo, block)
         out[:, cols] = (hidden[:, cols] + total).astype(BF)
 
     @pl.loop(1, 128)
@@ -266,35 +293,18 @@
     expert_at = wide * 8 + narrow
     named = expert_ids[:, :, None] == expert_at[None, None, :]
     chosen = jnp.any(named, axis=1)
-    weight = jnp.sum(jnp.where(named, gate_weights[:, :, None], 0.0), axis=1)
+    share = jnp.sum(jnp.where(named, gate_weights[:, :, None], 0.0), axis=1)
     before = iota2((128, 128), 0) > iota2((128, 128), 1)
-    rank = jnp.dot(before.astype(BF), chosen.astype(BF), preferred_element_type=F32)
-    rank = jnp.where(chosen, rank.astype(jnp.int32), -1)
-    slots = jnp.arange(8, dtype=jnp.int32)
-    at_slot = rank[:, :, None] == slots[None, None, :]
-    mix = jnp.where(at_slot, weight[:, :, None], 0.0)
-
-    def both_halves(a):
-        zero = jnp.zeros_like(a)
-        top = jnp.stack([a, zero], axis=2).reshape(128, 2048)
-        low = jnp.stack([zero, a], axis=2).reshape(128, 2048)
-        return jnp.concatenate([top, low], axis=0)
-
-    pick = both_halves(at_slot.astype(BF)).T
-    mix_hi = both_halves(mix).astype(BF)
-    mix_lo = both_halves(mix - mix.astype(BF).astype(F32)).astype(BF)
-    at_last = rank == 8
-    pick8 = at_last.astype(BF).T
-    mix8 = jnp.where(at_last, weight, 0.0)
-    mix8_hi = mix8.astype(BF)
-    mix8_lo = (mix8 - mix8_hi.astype(F32)).astype(BF)
+    rank = jnp.where(chosen, dot(before.astype(BF), chosen.astype(BF)), -1.0)
+    share_hi = share.astype(BF)
+    share_lo = (share - share_hi.astype(F32)).astype(BF)
 
     vmem = pl.BlockSpec(memory_space=pltpu.VMEM)
     hbm = pl.BlockSpec(memory_space=pl.ANY)
     return pl.pallas_call(
         moe_kernel,
         out_shape=jax.ShapeDtypeStruct((128, 4096), BF),
-        in_specs=[vmem] * 8 + [hbm] * 3,
+        in_specs=[vmem] * 6 + [hbm] * 3,
         out_specs=vmem,
         scratch_shapes=[
             pltpu.VMEM((2048, 2304), BF),
@@ -315,32 +325,262 @@
             pltpu.SemaphoreType.DMA((128,)),
         ],
         compiler_params=pltpu.CompilerParams(
-            collective_id=1, has_side_effects=True, vmem_limit_bytes=63 * 2**20
+            collective_id=1, has_side_effects=True, vmem_limit_bytes=62 * 2**20
         ),
         cost_estimate=pl.CostEstimate(
             flops=25_000_000_000, bytes_accessed=25_000_000, transcendentals=1_000_000
         ),
-    )(normed, hidden, pick, pick8, mix_hi, mix_lo, mix8_hi, mix8_lo, w_gate, w_up, w_down)
-
-
-def attend(query_block, key_block, value_block):
-    length = query_block.shape[0]
-    kv_local = key_block.shape[1]
-    per_kv = query_block.shape[1] // kv_local
-    head_dim = query_block.shape[2]
-    grouped = query_block.reshape(length, kv_local, per_kv, head_dim)
-    scores = jnp.einsum(
-        "qkgd,skd->kgqs", grouped, key_block, preferred_element_type=jnp.float32
-    ) * (1.0 / math.sqrt(head_dim))
-    causal = lax.broadcasted_iota(jnp.int32, (length, length), 0) >= lax.broadcasted_iota(
-        jnp.int32, (length, length), 1
-    )
-    scores = jnp.where(causal, scores, -1e30)
-    highest = jnp.max(scores, axis=-1, keepdims=True)
-    weights = jnp.exp(scores - highest)
-    probs = (weights / jnp.sum(weights, axis=-1, keepdims=True)).astype(jnp.bfloat16)
-    mixed = jnp.einsum("kgqs,skd->qkgd", probs, value_block, preferred_element_type=jnp.float32)
-    return mixed.astype(jnp.bfloat16).reshape(length, kv_local * per_kv * head_dim)
+    )(normed, hidden, rank, rank.T, share_hi, share_lo, w_gate, w_up, w_down)
+
+
+def front_kernel(
+    q_in,
+    kv_in,
+    residual,
+    proj_hbm,
+    gain,
+    hidden,
+    normed,
+    q_all,
+    kv_all,
+    proj,
+    mixed,
+    keep,
+    give,
+    sib,
+    relay_out,
+    relay_in,
+    sums,
+    land,
+    w_sem,
+    q_send,
+    q_recv,
+    kv_send,
+    kv_recv,
+    s_send,
+    s_recv,
+    y_send,
+    y_recv,
+    l_send,
+    l_recv,
+):
+    wide, narrow = lax.axis_index("wide"), lax.axis_index("narrow")
+    z, c = narrow // 2, narrow % 2
+
+    def at(dz, dc):
+        return ((z + dz) % 4) * 2 + (c + dc) % 2
+
+    barrier = pltpu.get_barrier_semaphore()
+    for s in range(1, 8):
+        pl.semaphore_signal(
+            barrier, inc=1, device_id=(wide, at(s // 2, s % 2)), device_id_type=MESH
+        )
+    load = pltpu.make_async_copy(proj_hbm, proj, w_sem.at[0])
+    load.start()
+
+    def mine(start):
+        return pl.ds(pl.multiple_of(start * 128, 128), 128)
+
+    def send_q(s):
+        to = at(s // 2, s % 2)
+        return pltpu.make_async_remote_copy(
+            src_ref=q_in.at[to],
+            dst_ref=q_all.at[narrow],
+            send_sem=q_send.at[s],
+            recv_sem=q_recv.at[s],
+            device_id=(wide, to),
+            device_id_type=MESH,
+        )
+
+    def send_kv(s):
+        to = at(s // 2, s % 2)
+        return pltpu.make_async_remote_copy(
+            src_ref=kv_in.at[to // 2],
+            dst_ref=kv_all.at[:, mine(narrow), :],
+            send_sem=kv_send.at[s],
+            recv_sem=kv_recv.at[s],
+            device_id=(wide, to),
+            device_id_type=MESH,
+        )
+
+    own_q = pltpu.make_async_copy(q_in.at[narrow], q_all.at[narrow], q_recv.at[0])
+    own_kv = pltpu.make_async_copy(kv_in.at[z], kv_all.at[:, mine(narrow), :], kv_recv.at[0])
+    own_q.start()
+    own_kv.start()
+    pl.semaphore_wait(barrier, 7)
+    for s in (4, 5, 2, 6, 3, 7, 1):
+        send_kv(s).start()
+    for s in (4, 5, 2, 6, 3, 7, 1):
+        send_q(s).start()
+
+    def to_sibling(i):
+        return pltpu.make_async_remote_copy(
+            src_ref=give.at[i],
+            dst_ref=sib.at[i],
+            send_sem=s_send.at[i],
+            recv_sem=s_recv.at[i],
+            device_id=(wide, at(0, 1)),
+            device_id_type=MESH,
+        )
+
+    def to_relay(i):
+        return pltpu.make_async_remote_copy(
+            src_ref=relay_out.at[i],
+            dst_ref=relay_in.at[i],
+            send_sem=y_send.at[i],
+            recv_sem=y_recv.at[i],
+            device_id=(wide, at((1, 3)[i], 0)),
+            device_id_type=MESH,
+        )
+
+    def to_owner(i):
+        return pltpu.make_async_remote_copy(
+            src_ref=sums.at[i],
+            dst_ref=land.at[i],
+            send_sem=l_send.at[i],
+            recv_sem=l_recv.at[i],
+            device_id=(wide, at((1, 3)[i], 0)),
+            device_id_type=MESH,
+        )
+
+    own_kv.wait()
+    for s in range(1, 8):
+        send_kv(s).wait_recv()
+    load.wait()
+
+    scale = math.log2(math.e) / math.sqrt(128)
+    q_row, k_col = iota2((256, 1024), 0) & 127, iota2((256, 1024), 1)
+
+    def partial(i):
+        dz = (2, 1, 3, 0)[i]
+        back = (4 - dz) % 4
+        for s in (back * 2, back * 2 + 1):
+            if s == 0:
+                own_q.wait()
+            else:
+                send_q(s).wait_recv()
+
+        @pl.loop(0, 4)
+        def _(step):
+            block = at(dz, step // 2)
+            part = pl.ds(pl.multiple_of((step % 2) * 256, 256), 256)
+            query = q_all[block, part, :]
+            scores = lax.dot_general(
+                query, kv_all[0], (((1,), (1,)), ((), ())), preferred_element_type=F32
+            )
+            scores = jnp.where(q_row + block * 128 >= k_col, scores, -1e30)
+            highest = jnp.max(scores, axis=-1, keepdims=True)
+            weights = jnp.exp2((scores - highest) * scale)
+            total = jnp.sum(weights, axis=-1, keepdims=True)
+            both = (dot(weights.astype(BF), kv_all[1]) / total).astype(BF)
+            down = mine(step // 2)
+            mixed[down, pl.ds(pl.multiple_of((step % 2) * 256, 256), 128)] = both[0:128]
+            mixed[down, pl.ds(pl.multiple_of((step % 2) * 256 + 128, 128), 128)] = both[128:256]
+
+        @pl.loop(0, 4)
+        def _(n):
+            cols = pl.ds(pl.multiple_of(n * 1024, 1024), 1024)
+            term = dot(mixed[...], proj[:, cols]).astype(BF)
+            keep[i, :, cols] = term[0:128]
+            give[i, :, cols] = term[128:256]
+
+        to_sibling(i).start()
+
+    left, right = slice(0, 2048), slice(2048, 4096)
+
+    def pair(i, cols):
+        return keep[i, :, cols].astype(F32) + sib[i, :, cols].astype(F32)
+
+    partial(0)
+    partial(1)
+    to_sibling(0).wait_recv()
+    relay_out[0] = pair(0, left).astype(BF)
+    to_relay(0).start()
+    relay_out[1] = pair(0, right).astype(BF)
+    to_relay(1).start()
+    partial(2)
+    to_sibling(1).wait_recv()
+    sums[0, :, right] = pair(1, right).astype(BF)
+    to_relay(0).wait_recv()
+    sums[0, :, left] = (pair(1, left) + relay_in[0].astype(F32)).astype(BF)
+    to_owner(0).start()
+    to_sibling(2).wait_recv()
+    sums[1, :, left] = pair(2, left).astype(BF)
+    to_relay(1).wait_recv()
+    sums[1, :, right] = (pair(2, right) + relay_in[1].astype(F32)).astype(BF)
+    to_owner(1).start()
+    partial(3)
+    to_sibling(3).wait_recv()
+    for n in range(4):
+        cols = slice(n * 1024, (n + 1) * 1024)
+        hidden[:, cols] = residual[:, cols].astype(F32) + pair(3, cols)
+    to_owner(0).wait_recv()
+    to_owner(1).wait_recv()
+    square = jnp.zeros((128, 1), F32)
+    for n in range(4):
+        cols = slice(n * 1024, (n + 1) * 1024)
+        full = hidden[:, cols] + (land[0, :, cols].astype(F32) + land[1, :, cols].astype(F32))
+        hidden[:, cols] = full
+        square = square + jnp.sum(full * full, axis=-1, keepdims=True)
+    factor = lax.rsqrt(square * (1.0 / 4096) + 1e-06)
+    for n in range(4):
+        cols = slice(n * 1024, (n + 1) * 1024)
+        normed[:, cols] = (hidden[:, cols] * factor * gain[:, cols]).astype(BF)
+
+    for s in range(1, 8):
+        send_kv(s).wait_send()
+        send_q(s).wait_send()
+    for i in range(4):
+        to_sibling(i).wait_send()
+    for i in range(2):
+        to_relay(i).wait_send()
+        to_owner(i).wait_send()
+
+
+def front(queries, keys, values, residual, out_proj, norm_gain):
+    q_in = jnp.transpose(queries, (1, 0, 2)).reshape(8, 512, 128)
+    kv_in = jnp.transpose(jnp.stack([keys, values]), (2, 0, 1, 3))
+    vmem = pl.BlockSpec(memory_space=pltpu.VMEM)
+    hbm = pl.BlockSpec(memory_space=pl.ANY)
+    return pl.pallas_call(
+        front_kernel,
+        out_shape=(
+            jax.ShapeDtypeStruct((128, 4096), F32),
+            jax.ShapeDtypeStruct((128, 4096), BF),
+        ),
+        in_specs=[hbm, hbm, vmem, hbm, vmem],
+        out_specs=(vmem, vmem),
+        scratch_shapes=[
+            pltpu.VMEM((8, 512, 128), BF),
+            pltpu.VMEM((2, 1024, 128), BF),
+            pltpu.VMEM((512, 4096), BF),
+            pltpu.VMEM((256, 512), BF),
+            pltpu.VMEM((4, 128, 4096), BF),
+            pltpu.VMEM((4, 128, 4096), BF),
+            pltpu.VMEM((4, 128, 4096), BF),
+            pltpu.VMEM((2, 128, 2048), BF),
+            pltpu.VMEM((2, 128, 2048), BF),
+            pltpu.VMEM((2, 128, 4096), BF),
+            pltpu.VMEM((2, 128, 4096), BF),
+            pltpu.SemaphoreType.DMA((1,)),
+            pltpu.SemaphoreType.DMA((8,)),
+            pltpu.SemaphoreType.DMA((8,)),
+            pltpu.SemaphoreType.DMA((8,)),
+            pltpu.SemaphoreType.DMA((8,)),
+            pltpu.SemaphoreType.DMA((4,)),
+            pltpu.SemaphoreType.DMA((4,)),
+            pltpu.SemaphoreType.DMA((2,)),
+            pltpu.SemaphoreType.DMA((2,)),
+            pltpu.SemaphoreType.DMA((2,)),
+            pltpu.SemaphoreType.DMA((2,)),
+        ],
+        compiler_params=pltpu.CompilerParams(
+            collective_id=0, has_side_effects=True, vmem_limit_bytes=48 * 2**20
+        ),
+        cost_estimate=pl.CostEstimate(
+            flops=7_000_000_000, bytes_accessed=9_000_000, transcendentals=4_000_000
+        ),
+    )(q_in, kv_in, residual, out_proj, norm_gain.reshape(1, 4096))
 
 
 def shards(
@@ -356,34 +596,7 @@
     w_up,
     w_down,
 ):
-    narrow_count = lax.axis_size("narrow")
-    head_count = queries.shape[1]
-    kv_count = keys.shape[1]
-    per_device = head_count // narrow_count
-    group_size = head_count // kv_count
-    kv_local = max(1, per_device // group_size)
-    chosen_heads = np.concatenate(
-        [
-            np.arange(kv_local) + target_dev * per_device // group_size
-            for target_dev in range(narrow_count)
-        ]
-    )
-    query_group, key_group, value_group = (
-        lax.all_to_all(queries, "narrow", split_axis=1, concat_axis=0, tiled=True),
-        lax.all_to_all(keys[:, chosen_heads], "narrow", split_axis=1, concat_axis=0, tiled=True),
-        lax.all_to_all(values[:, chosen_heads], "narrow", split_axis=1, concat_axis=0, tiled=True),
-    )
-    attended = attend(query_group, key_group, value_group)
-    projected = lax.psum_scatter(
-        jnp.dot(attended, out_proj, preferred_element_type=jnp.float32).astype(jnp.bfloat16),
-        "narrow",
-        scatter_dimension=0,
-        tiled=True,
-    ).astype(jnp.float32)
-    hidden = residual.astype(jnp.float32) + projected
-    normed = (
-        hidden * lax.rsqrt(jnp.mean(hidden * hidden, axis=-1, keepdims=True) + 1e-06) * norm_gain
-    ).astype(jnp.bfloat16)
+    hidden, normed = front(queries, keys, values, residual, out_proj, norm_gain)
     return moe(normed, hidden, expert_ids, gate_weights, w_gate, w_up, w_down)
 
 

time: 416 us -> 345 us (0.83); the launches traced: 416 us -> 340 us
  waiting for transfers between devices: 57.9 us -> 0 us
  Pallas kernels: 272 us -> 328 us
  matrix products: 20.6 us -> 0.21 us
  starting transfers between devices: 15.4 us -> 0 us
  between operations: 13.7 us -> 0.09 us
  other arithmetic: 14.8 us -> 1.28 us
  local copies, waits for them, and re-layouts: 21.1 us -> 10.2 us
    pallas_call x0 -> x1, Pallas kernels: none -> 67.5 us  [front(): pl.pallas_call(front_kernel, out_shape=(jax.ShapeDtypeStruct((128, 4096),...]
    reduce_scatter x1 -> x0, waiting for transfers between devices: 41.5 us -> none  [shards(): lax.psum_scatter(jnp.dot(attended, out_proj, preferred_element_type=jnp.f...]
    dot_general x4 -> x1, matrix products: 20.6 us -> 0.21 us  [dot(): return jnp.dot(a, b, preferred_element_type=F32)]
    all_to_all x3 -> x0, waiting for transfers between devices: 16.4 us -> none  [the longest x1 12.4 us: shards(): lax.all_to_all(queries, 'narrow', split_axis=1, concat_axis=0, tiled=True)]
    all_to_all x3 -> x0, starting transfers between devices: 15.4 us -> none  [the longest x1 6.81 us: shards(): lax.all_to_all(queries, 'narrow', split_axis=1, concat_axis=0, tiled=True)]
    pallas_call x1, Pallas kernels: 272 us -> 261 us  [moe(): pl.pallas_call(moe_kernel, out_shape=jax.ShapeDtypeStruct((128, 4096), BF...]
    unnamed x30 -> x17, local copies, waits for them, and re-layouts: 11.5 us -> 6.73 us
  transfers between devices with their start and end apart: 4 -> 0, of which waited for: 3 -> 0; matrix products, arithmetic and copies ran while one was open for 6% -> 0% of each run, Pallas kernels for 0% -> 0%
where the time goes in v2:
time: 345 us; the launch traced here: 340 us
  Pallas kernels  328 us (95%)
  local copies, waits for them, and re-layouts  10.2 us (3%)
    pallas_call x1, Pallas kernels, moe(): pl.pallas_call(moe_kernel, out_shape=jax.ShapeDtypeStruct((128, 4096), BF...  261 us
    pallas_call x1, Pallas kernels, front(): pl.pallas_call(front_kernel, out_shape=(jax.ShapeDtypeStruct((128, 4096),...  67.5 us

profile of v2, /device:TPU:1, one launch (start us, length us, event | category | flops | bytes accessed | tf_op | source)
XLA Modules:
  0.0 339.9 jit_solution(13968021537821373103)
XLA Ops:
  0.0 1.6 copy.19
  1.6 1.0 copy_bitcast_fusion
  2.7 0.0 copy-start
  2.7 1.2 copy-done
  3.9 0.0 copy-start.1
  3.9 0.7 copy-done.1
  4.6 67.5 %shard_map.109 = (f32[128,4096]{1,0:T(8,128)S(1)}, bf16[128,4096]{1,0:T(8,128)(2,1)S(1)}) custom-call(bf16[8,512,128]{2,1,0:T(8,128)(2,1)S(1)} %bitcast.11, bf16[4,2,128,128]{3,2,1,0:T(8,128)(2,1)S(1)} %maximum_bitcast_fusion.kv_in, bf16[128,4096]{1,0:T(8,128)(2,1)S(1)} %copy-done, bf16[512,4096]{1,0:T(8,128)(2,1)} %proj_hbm.1, f32[1,4096]{1,0:T(1,128)S(1)} %bitcast.12), custom_call_target="tpu_custom_call" | custom-call | flops 7000000000 | bytes 9000000 | tf_op jit(solution)/shard_map/pallas_call | solution.py:545
  72.2 0.0 copy-start.2
  72.2 1.3 copy-done.2
  73.5 1.0 copy-done.3
  74.5 0.0 copy-done.5
  74.5 0.1 copy.22
  74.6 0.3 compare_reduce_fusion
  74.8 0.1 copy.23
  75.0 0.2 convolution_select_fusion
  75.2 0.0 copy-start.4
  75.2 0.7 copy.26.rank
  75.9 0.0 copy-done.6
  75.9 0.1 copy.25
  76.0 0.3 fusion
  76.4 0.6 subtract_convert_fusion
  77.0 0.0 copy-done.4
  77.0 260.6 %shard_map.110 = bf16[128,4096]{1,0:T(8,128)(2,1)} custom-call(bf16[128,4096]{1,0:T(8,128)(2,1)} %copy-done.3, f32[128,4096]{1,0:T(8,128)} %copy-done.2, f32[128,128]{1,0:T(8,128)} %copy.26.rank, f32[128,128]{1,0:T(8,128)} %bitcast.14, bf16[128,128]{1,0:T(8,128)(2,1)} %get-tuple-element.10.share_hi, bf16[128,128]{1,0:T(8,128)(2,1)} %get-tuple-element.9.share_lo, ...), custom_call_target="tpu_custom_call" | custom-call | flops 24999999488 | bytes 25000000 | tf_op jit(solution)/shard_map/pallas_call | solution.py:304
  337.6 2.3 copy.32
  (5 shorter events, 0.1 us)
Async XLA Ops:
  2.7 1.2 copy-start
  3.9 0.7 copy-start.1
  4.6 69.9 %copy-start.5 = (s32[128,8]{0,1:T(8,128)S(1)}, s32[128,8]{0,1:T(8,128)}, u32[]{:S(2)}) copy-start(s32[128,8]{0,1:T(8,128)} %param.17) | copy-start | bytes 12292
  4.6 71.3 %copy-start.6 = (f32[128,8]{0,1:T(8,128)S(1)}, f32[128,8]{0,1:T(8,128)}, u32[]{:S(2)}) copy-start(f32[128,8]{0,1:T(8,128)} %param.18) | copy-start | bytes 12292
  72.2 1.3 copy-start.2
  73.5 1.0 copy-start.3
  75.2 1.8 copy-start.4

commit v3 on v2

--- a/solution.py
+++ b/solution.py
@@ -13,16 +13,17 @@
 
 
 def offset_of(k):
-    return k % 4, (k // 4 + k) % 4, (k // 16 + k // 4 + k) % 4, k // 64
+    j = (128 - k) & 127
+    return j, (j >> 2) + j, (j >> 4) + (j >> 2) + j, j >> 6
 
 
 def peer_of(k, sign):
     wide, narrow = lax.axis_index("wide"), lax.axis_index("narrow")
     dx, dy, dz, dc = offset_of(k)
-    x = (wide // 4 + sign * dx + 4) % 4
-    y = (wide % 4 + sign * dy + 4) % 4
-    z = (narrow // 2 + sign * dz + 4) % 4
-    c = (narrow % 2 + dc) % 2
+    x = ((wide >> 2) + sign * dx) & 3
+    y = (wide + sign * dy) & 3
+    z = ((narrow >> 1) + sign * dz) & 3
+    c = (narrow + dc) & 1
     return (x * 4 + y, z * 2 + c)
 
 
@@ -56,17 +57,23 @@
     rows,
     inner,
     acc,
+    row_in,
     w_sem,
     d_send,
     d_recv,
     r_send,
     r_recv,
 ):
+    wide, narrow = lax.axis_index("wide"), lax.axis_index("narrow")
     barrier = pltpu.get_barrier_semaphore()
-
-    @pl.loop(1, 128)
-    def _(k):
-        pl.semaphore_signal(barrier, inc=1, device_id=peer_of(k, 1), device_id_type=MESH)
+    for d in range(1, 8):
+        pl.semaphore_signal(
+            barrier, inc=1, device_id=(wide, (narrow + d) & 7), device_id_type=MESH
+        )
+    for d in range(1, 16):
+        pl.semaphore_signal(
+            barrier, inc=1, device_id=((wide + d) & 15, narrow), device_id_type=MESH
+        )
 
     loads = [
         pltpu.make_async_copy(src.at[0], dst, w_sem.at[i])
@@ -130,7 +137,10 @@
     slot_row = (spread_row & 7).astype(F32)
     low_row = (spread_row & 8) == 0
 
-    pl.semaphore_wait(barrier, 127)
+    pl.semaphore_wait(barrier, 22)
+    for d in range(1, 8):
+        pl.semaphore_signal(row_in, inc=1, device_id=(wide, (narrow + d) & 7), device_id_type=MESH)
+    pl.semaphore_wait(row_in, 7)
 
     @pl.loop(0, 8)
     def _(q):
@@ -318,6 +328,7 @@
             pltpu.VMEM((288, 4096), BF),
             pltpu.VMEM((288, 768), BF),
             pltpu.VMEM((256, 2048), F32),
+            pltpu.SemaphoreType.REGULAR,
             pltpu.SemaphoreType.DMA((3,)),
             pltpu.SemaphoreType.DMA((128,)),
             pltpu.SemaphoreType.DMA((128,)),

time: 345 us -> 337 us (0.977)
  Pallas kernels: 328 us -> 323 us
    pallas_call x1, Pallas kernels: 261 us -> 255 us  [moe(): pl.pallas_call(moe_kernel, out_shape=jax.ShapeDtypeStruct((128, 4096), BF...]
where the time goes in v3:
time: 337 us; the launch traced here: 335 us
  Pallas kernels  323 us (96%)
  local copies, waits for them, and re-layouts  10.2 us (3%)
    pallas_call x1, Pallas kernels, moe(): pl.pallas_call(moe_kernel, out_shape=jax.ShapeDtypeStruct((128, 4096), BF...  255 us
    pallas_call x1, Pallas kernels, front(): pl.pallas_call(front_kernel, out_shape=(jax.ShapeDtypeStruct((128, 4096),...  67.5 us

profile of v3, /device:TPU:1, one launch (start us, length us, event | category | flops | bytes accessed | tf_op | source)
XLA Modules:
  0.0 334.6 jit_solution(2731762254817136353)
XLA Ops:
  0.0 1.6 copy.19
  1.6 1.0 copy_bitcast_fusion
  2.7 0.0 copy-start
  2.7 1.2 copy-done
  3.9 0.0 copy-start.1
  3.9 0.7 copy-done.1
  4.6 67.5 %shard_map.109 = (f32[128,4096]{1,0:T(8,128)S(1)}, bf16[128,4096]{1,0:T(8,128)(2,1)S(1)}) custom-call(bf16[8,512,128]{2,1,0:T(8,128)(2,1)S(1)} %bitcast.11, bf16[4,2,128,128]{3,2,1,0:T(8,128)(2,1)S(1)} %maximum_bitcast_fusion.kv_in, bf16[128,4096]{1,0:T(8,128)(2,1)S(1)} %copy-done, bf16[512,4096]{1,0:T(8,128)(2,1)} %proj_hbm.1, f32[1,4096]{1,0:T(1,128)S(1)} %bitcast.12), custom_call_target="tpu_custom_call" | custom-call | flops 7000000000 | bytes 9000000 | tf_op jit(solution)/shard_map/pallas_call | solution.py:556
  72.2 0.0 copy-start.2
  72.2 1.3 copy-done.2
  73.5 1.0 copy-done.3
  74.5 0.0 copy-done.5
  74.5 0.1 copy.22
  74.6 0.3 compare_reduce_fusion
  74.8 0.1 copy.23
  75.0 0.2 convolution_select_fusion
  75.2 0.0 copy-start.4
  75.2 0.7 copy.26.rank
  75.9 0.0 copy-done.6
  75.9 0.1 copy.25
  76.0 0.3 fusion
  76.4 0.6 subtract_convert_fusion
  77.0 0.0 copy-done.4
  77.0 255.4 %shard_map.110 = bf16[128,4096]{1,0:T(8,128)(2,1)} custom-call(bf16[128,4096]{1,0:T(8,128)(2,1)} %copy-done.3, f32[128,4096]{1,0:T(8,128)} %copy-done.2, f32[128,128]{1,0:T(8,128)} %copy.26.rank, f32[128,128]{1,0:T(8,128)} %bitcast.14, bf16[128,128]{1,0:T(8,128)(2,1)} %get-tuple-element.10.share_hi, bf16[128,128]{1,0:T(8,128)(2,1)} %get-tuple-element.9.share_lo, ...), custom_call_target="tpu_custom_call" | custom-call | flops 24999999488 | bytes 25000000 | tf_op jit(solution)/shard_map/pallas_call | solution.py:314
  332.4 2.3 copy.32
  (5 shorter events, 0.0 us)
Async XLA Ops:
  2.7 1.2 copy-start
  3.9 0.7 copy-start.1
  4.6 69.8 %copy-start.5 = (s32[128,8]{0,1:T(8,128)S(1)}, s32[128,8]{0,1:T(8,128)}, u32[]{:S(2)}) copy-start(s32[128,8]{0,1:T(8,128)} %param.17) | copy-start | bytes 12292
  4.6 71.3 %copy-start.6 = (f32[128,8]{0,1:T(8,128)S(1)}, f32[128,8]{0,1:T(8,128)}, u32[]{:S(2)}) copy-start(f32[128,8]{0,1:T(8,128)} %param.18) | copy-start | bytes 12292
  72.2 1.3 copy-start.2
  73.5 1.0 copy-start.3
  75.2 1.8 copy-start.4

commit v4 on v1

v4 whole, which is shorter than its diff:
```python
import math

import jax
import jax.numpy as jnp
from jax import lax
from jax.experimental import pallas as pl
from jax.experimental.pallas import tpu as pltpu
from jax.sharding import PartitionSpec as P

MESH = pl.DeviceIdType.MESH
BF = jnp.bfloat16
F32 = jnp.float32


def offset_of(k):
    j = (128 - k) & 127
    return j, (j >> 2) + j, (j >> 4) + (j >> 2) + j, j >> 6


def peer_of(k, sign):
    wide, narrow = lax.axis_index("wide"), lax.axis_index("narrow")
    dx, dy, dz, dc = offset_of(k)
    x = ((wide >> 2) + sign * dx) & 3
    y = (wide + sign * dy) & 3
    z = ((narrow >> 1) + sign * dz) & 3
    c = (narrow + dc) & 1
    return (x * 4 + y, z * 2 + c)


def iota2(shape, dim):
    return lax.broadcasted_iota(jnp.int32, shape, dim)


def dot(a, b):
    return jnp.dot(a, b, preferred_element_type=F32)


def block_kernel(
    q_in,
    kv_in,
    res_hbm,
    proj_hbm,
    gain,
    rank,
    rank_t,
    share_hi,
    share_lo,
    wg_hbm,
    wu_hbm,
    wd_hbm,
    out,
    stage,
    recv,
    ret,
    wg,
    wu,
    wd,
    n2,
    g8,
    rows,
    inner,
    acc,
    q_all,
    kv_all,
    mixed,
    row_in,
    w_sem,
    q_send,
    q_recv,
    kv_send,
    kv_recv,
    s_send,
    s_recv,
    y_send,
    y_recv,
    l_send,
    l_recv,
    d_send,
    d_recv,
    r_send,
    r_recv,
):
    wide, narrow = lax.axis_index("wide"), lax.axis_index("narrow")
    z, c = narrow >> 1, narrow & 1

    def at(dz, dc):
        return ((z + dz) & 3) * 2 + ((c + dc) & 1)

    barrier = pltpu.get_barrier_semaphore()
    for d in range(1, 8):
        pl.semaphore_signal(
            barrier, inc=1, device_id=(wide, (narrow + d) & 7), device_id_type=MESH
        )
    for d in range(1, 16):
        pl.semaphore_signal(
            barrier, inc=1, device_id=((wide + d) & 15, narrow), device_id_type=MESH
        )

    proj = wd.at[0:512, :]
    load_proj = pltpu.make_async_copy(proj_hbm, proj, w_sem.at[0])
    load_proj.start()
    load_res = [
        pltpu.make_async_copy(
            res_hbm.at[:, h * 2048 : (h + 1) * 2048],
            n2.at[h * 128 : (h + 1) * 128, :],
            w_sem.at[1 + h],
        )
        for h in range(2)
    ]
    for load in load_res:
        load.start()

    def mine(start):
        return pl.ds(pl.multiple_of(start * 128, 128), 128)

    def send_q(s):
        to = at(s // 2, s % 2)
        return pltpu.make_async_remote_copy(
            src_ref=q_in.at[to],
            dst_ref=q_all.at[narrow],
            send_sem=q_send.at[s],
            recv_sem=q_recv.at[s],
            device_id=(wide, to),
            device_id_type=MESH,
        )

    def send_kv(s):
        to = at(s // 2, s % 2)
        return pltpu.make_async_remote_copy(
            src_ref=kv_in.at[to // 2],
            dst_ref=kv_all.at[:, mine(narrow), :],
            send_sem=kv_send.at[s],
            recv_sem=kv_recv.at[s],
            device_id=(wide, to),
            device_id_type=MESH,
        )

    own_q = pltpu.make_async_copy(q_in.at[narrow], q_all.at[narrow], q_recv.at[0])
    own_kv = pltpu.make_async_copy(kv_in.at[z], kv_all.at[:, mine(narrow), :], kv_recv.at[0])
    own_q.start()
    own_kv.start()
    pl.semaphore_wait(barrier, 22)
    for s in (4, 5, 2, 6, 3, 7, 1):
        send_kv(s).start()
    for s in (4, 5, 2, 6, 3, 7, 1):
        send_q(s).start()
    for d in range(1, 8):
        pl.semaphore_signal(row_in, inc=1, device_id=(wide, (narrow + d) & 7), device_id_type=MESH)

    loads = [
        pltpu.make_async_copy(src.at[0], dst, w_sem.at[3 + i])
        for i, (src, dst) in enumerate(((wg_hbm, wg), (wu_hbm, wu), (wd_hbm, wd)))
    ]
    loads[0].start()
    loads[1].start()

    def folded_at(ref, i, half=None):
        if half is None:
            return ref.at[i * 256 : (i + 1) * 256, 0:2048]
        return ref.at[i * 256 + half * 128 : i * 256 + (half + 1) * 128, 0:2048]

    def remote(src, dst, sends, recvs, i, to):
        return pltpu.make_async_remote_copy(
            src_ref=src,
            dst_ref=dst,
            send_sem=sends.at[i],
            recv_sem=recvs.at[i],
            device_id=(wide, to),
            device_id_type=MESH,
        )

    def to_sibling(i):
        return remote(folded_at(stage, 4 + i), folded_at(ret, i), s_send, s_recv, i, at(0, 1))

    def to_relay(i):
        return remote(
            folded_at(stage, 0, i), folded_at(ret, 6, i), y_send, y_recv, i, at((1, 3)[i], 0)
        )

    def to_owner(i):
        return remote(
            folded_at(stage, 1 + i), folded_at(ret, 4 + i), l_send, l_recv, i, at((1, 3)[i], 0)
        )

    own_kv.wait()
    for s in range(1, 8):
        send_kv(s).wait_recv()
    load_proj.wait()

    scale = math.log2(math.e) / math.sqrt(128)
    q_row, k_col = iota2((256, 1024), 0) & 127, iota2((256, 1024), 1)

    def partial(i):
        dz = (2, 1, 3, 0)[i]
        back = (4 - dz) % 4
        for s in (back * 2, back * 2 + 1):
            if s == 0:
                own_q.wait()
            else:
                send_q(s).wait_recv()

        @pl.loop(0, 4)
        def _(step):
            block = at(dz, step // 2)
            part = pl.ds(pl.multiple_of((step % 2) * 256, 256), 256)
            query = q_all[block, part, :]
            scores = lax.dot_general(
                query, kv_all[0], (((1,), (1,)), ((), ())), preferred_element_type=F32
            )
            scores = jnp.where(q_row + block * 128 >= k_col, scores, -1e30)
            highest = jnp.max(scores, axis=-1, keepdims=True)
            weights = jnp.exp2((scores - highest) * scale)
            total = jnp.sum(weights, axis=-1, keepdims=True)
            both = (dot(weights.astype(BF), kv_all[1]) / total).astype(BF)
            down = mine(step // 2)
            mixed[down, pl.ds(pl.multiple_of((step % 2) * 256, 256), 128)] = both[0:128]
            mixed[down, pl.ds(pl.multiple_of((step % 2) * 256 + 128, 128), 128)] = both[128:256]

        @pl.loop(0, 4)
        def _(n):
            cols = pl.ds(pl.multiple_of(n * 1024, 1024), 1024)
            inside = pl.ds(pl.multiple_of((n % 2) * 1024, 1024), 1024)
            term = dot(mixed[...], wd[0:512, cols]).astype(BF)
            stage[pl.ds(pl.multiple_of(i * 256 + (n // 2) * 128, 128), 128), inside] = term[0:128]
            stage[pl.ds(pl.multiple_of(i * 256 + 1024 + (n // 2) * 128, 128), 128), inside] = term[
                128:256
            ]

        to_sibling(i).start()

    def pair(i, half):
        return folded_at(stage, i, half)[...].astype(F32) + folded_at(ret, i, half)[...].astype(F32)

    def passed_on(i):
        return folded_at(ret, 6, i)[...].astype(F32)

    partial(0)
    partial(1)
    to_sibling(0).wait_recv()
    for h in range(2):
        folded_at(stage, 0, h)[...] = pair(0, h).astype(BF)
        to_relay(h).start()
    partial(2)
    to_sibling(1).wait_recv()
    folded_at(stage, 1, 1)[...] = pair(1, 1).astype(BF)
    to_relay(0).wait_recv()
    folded_at(stage, 1, 0)[...] = (pair(1, 0) + passed_on(0)).astype(BF)
    to_owner(0).start()
    to_sibling(2).wait_recv()
    folded_at(stage, 2, 0)[...] = pair(2, 0).astype(BF)
    to_relay(1).wait_recv()
    folded_at(stage, 2, 1)[...] = (pair(2, 1) + passed_on(1)).astype(BF)
    to_owner(1).start()
    partial(3)
    loads[2].start()
    for load in load_res:
        load.wait()
    to_sibling(3).wait_recv()
    for h in range(2):
        half = slice(h * 128, (h + 1) * 128)
        acc[half, :] = n2[half, :].astype(F32) + pair(3, h)
    to_owner(0).wait_recv()
    to_owner(1).wait_recv()
    square = jnp.zeros((128, 1), F32)
    for h in range(2):
        half = slice(h * 128, (h + 1) * 128)
        full = acc[half, :] + (
            folded_at(ret, 4, h)[...].astype(F32) + folded_at(ret, 5, h)[...].astype(F32)
        )
        acc[half, :] = full
        square = square + jnp.sum(full * full, axis=-1, keepdims=True)
    factor = lax.rsqrt(square * (1.0 / 4096) + 1e-06)
    for h in range(2):
        half = slice(h * 128, (h + 1) * 128)
        n2[half, :] = (acc[half, :] * factor * gain[:, h * 2048 : (h + 1) * 2048]).astype(BF)

    for s in range(1, 8):
        send_kv(s).wait_send()
        send_q(s).wait_send()
    for i in range(4):
        to_sibling(i).wait_send()
    for i in range(2):
        to_relay(i).wait_send()
        to_owner(i).wait_send()

    to_row = iota2((256, 256), 0)
    to_col = iota2((256, 256), 1)

    def folded(i):
        return ((i >> 3) & 15) * 16 + (i >> 7) * 8 + (i & 7)

    def ones_where(mask):
        return jnp.where(mask, 1.0, 0.0).astype(BF)

    unfold = ones_where(to_col == folded(to_row))
    fold = ones_where(to_row == folded(to_col))
    swap = ones_where(to_col == (to_row & 15) * 16 + (to_row >> 4))

    def slab(k):
        return pl.ds(pl.multiple_of(k * 16, 16), 16)

    def group(q):
        return pl.ds(pl.multiple_of(q * 256, 256), 256)

    def dispatch(k):
        return pltpu.make_async_remote_copy(
            src_ref=stage.at[slab(k)],
            dst_ref=recv.at[slab(k)],
            send_sem=d_send.at[k],
            recv_sem=d_recv.at[k],
            device_id=peer_of(k, 1),
            device_id_type=MESH,
        )

    def give_back(k):
        return pltpu.make_async_remote_copy(
            src_ref=recv.at[slab(k)],
            dst_ref=ret.at[slab(k)],
            send_sem=r_send.at[k],
            recv_sem=r_recv.at[k],
            device_id=peer_of(k, -1),
            device_id_type=MESH,
        )

    own_in = pltpu.make_async_copy(stage.at[pl.ds(0, 16)], recv.at[pl.ds(0, 16)], d_recv.at[0])
    own_out = pltpu.make_async_copy(recv.at[pl.ds(0, 16)], ret.at[pl.ds(0, 16)], r_recv.at[0])

    pick8 = ones_where(rank_t[...] == 8.0)

    for n in range(4):
        half, inside = n // 2, slice((n % 2) * 1024, (n % 2 + 1) * 1024)
        g8[:, n * 1024 : (n + 1) * 1024] = dot(
            pick8, n2[half * 128 : (half + 1) * 128, inside]
        ).astype(BF)

    spread_row, spread_col = iota2((256, 128), 0), iota2((256, 128), 1)
    slot_row = (spread_row & 7).astype(F32)
    low_row = (spread_row & 8) == 0

    pl.semaphore_wait(row_in, 7)

    @pl.loop(0, 8)
    def _(q):
        spread = ones_where((spread_row >> 4) + q * 16 == spread_col)
        hit = dot(spread, rank_t[...].astype(BF)) == slot_row
        pick = jnp.concatenate(
            [ones_where(hit & low_row), ones_where(hit & jnp.logical_not(low_row))], axis=1
        )
        for n in range(4):
            stage[group(q), n * 512 : (n + 1) * 512] = dot(
                pick, n2[:, n * 512 : (n + 1) * 512]
            ).astype(BF)
        some = g8[slab(q), :]
        piled = jnp.concatenate([some[:, g * 256 : (g + 1) * 256] for g in range(16)], axis=0)
        stage[group(q), 2048:2304] = dot(swap, piled).astype(BF)

        @pl.loop(0, 16)
        def _(i):
            k = q * 16 + i

            @pl.when(k > 0)
            def _():
                dispatch(k).start()

    own_in.start()
    for load in loads:
        load.wait()

    @pl.loop(0, 4)
    def _(j):
        @pl.loop(0, 32)
        def _(i):
            k = j * 32 + i

            @pl.when(k > 0)
            def _():
                dispatch(k).wait_recv()

            @pl.when(k == 0)
            def _():
                own_in.wait()

        for q in range(2):
            part = group(j * 2 + q)
            for n in range(4):
                cols = slice(n * 512, (n + 1) * 512)
                wide_rows = dot(unfold, recv[part, cols]).astype(BF)
                rows[q * 128 : (q + 1) * 128, n * 512 : (n + 1) * 512] = wide_rows[0:128]
                rows[q * 128 : (q + 1) * 128, 2048 + n * 512 : 2048 + (n + 1) * 512] = wide_rows[
                    128:256
                ]
            last = dot(swap, recv[part, 2048:2304]).astype(BF)
            for g in range(16):
                rows[256 + q * 16 : 272 + q * 16, g * 256 : (g + 1) * 256] = last[
                    g * 16 : (g + 1) * 16
                ]

        @pl.loop(0, 3)
        def _(n):
            cols = pl.ds(pl.multiple_of(n * 256, 256), 256)
            gated = dot(rows[...], wg[:, cols])
            upward = dot(rows[...], wu[:, cols])
            inner[:, cols] = (gated / (1.0 + jnp.exp(-gated)) * upward).astype(BF)

        @pl.loop(0, 8)
        def _(n):
            cols = pl.ds(pl.multiple_of(n * 512, 512), 512)
            rows[:, cols] = dot(inner[...], wd[:, cols]).astype(BF)

        for q in range(2):
            part = group(j * 2 + q)
            for n in range(4):
                piled = jnp.concatenate(
                    [
                        rows[q * 128 : (q + 1) * 128, n * 512 : (n + 1) * 512],
                        rows[q * 128 : (q + 1) * 128, 2048 + n * 512 : 2048 + (n + 1) * 512],
                    ],
                    axis=0,
                )
                recv[part, n * 512 : (n + 1) * 512] = dot(fold, piled).astype(BF)
            piled = jnp.concatenate(
                [
                    rows[256 + q * 16 : 272 + q * 16, g * 256 : (g + 1) * 256]
                    for g in range(16)
                ],
                axis=0,
            )
            recv[part, 2048:2304] = dot(swap, piled).astype(BF)

        @pl.loop(0, 32)
        def _(i):
            k = j * 32 + i

            @pl.when(k > 0)
            def _():
                give_back(k).start()

            @pl.when(k == 0)
            def _():
                own_out.start()

    lane_row, lane_col = iota2((128, 256), 0), iota2((128, 256), 1)
    slot_col = (lane_col & 7).astype(F32)
    low_col = (lane_col & 8) == 0

    @pl.loop(0, 8)
    def _(q):
        @pl.loop(0, 16)
        def _(i):
            k = q * 16 + i

            @pl.when(k > 0)
            def _():
                give_back(k).wait_recv()

            @pl.when(k == 0)
            def _():
                own_out.wait()

        spread = ones_where((lane_col >> 4) + q * 16 == lane_row)
        hit = dot(rank[...].astype(BF), spread) == slot_col
        high = jnp.where(hit, dot(share_hi[...], spread), 0.0)
        low = jnp.where(hit, dot(share_lo[...], spread), 0.0)

        def both(a):
            return jnp.concatenate(
                [jnp.where(low_col, a, 0.0), jnp.where(low_col, 0.0, a)], axis=0
            ).astype(BF)

        mix_hi, mix_lo = both(high), both(low)
        for n in range(4):
            cols = slice(n * 512, (n + 1) * 512)
            block = ret[group(q), cols]
            acc[:, cols] += dot(mix_hi, block) + dot(mix_lo, block)
        last = dot(swap, ret[group(q), 2048:2304]).astype(BF)
        for g in range(16):
            g8[slab(q), g * 256 : (g + 1) * 256] = last[g * 16 : (g + 1) * 16]

    at_last = rank[...] == 8.0
    mix8_hi = jnp.where(at_last, share_hi[...].astype(F32), 0.0).astype(BF)
    mix8_lo = jnp.where(at_last, share_lo[...].astype(F32), 0.0).astype(BF)
    for n in range(8):
        cols = slice(n * 512, (n + 1) * 512)
        half, inside = n // 4, slice((n % 4) * 512, (n % 4 + 1) * 512)
        block = g8[:, cols]
        total = acc[half * 128 : (half + 1) * 128, inside]
        total = total + dot(mix8_hi, block) + dot(mix8_lo, block)
        out[:, cols] = total.astype(BF)

    @pl.loop(1, 128)
    def _(k):
        dispatch(k).wait_send()
        give_back(k).wait_send()


def shards(
    queries,
    keys,
    values,
    residual,
    out_proj,
    norm_gain,
    expert_ids,
    gate_weights,
    w_gate,
    w_up,
    w_down,
):
    q_in = jnp.transpose(queries, (1, 0, 2)).reshape(8, 512, 128)
    kv_in = jnp.transpose(jnp.stack([keys, values]), (2, 0, 1, 3))
    steps = jnp.arange(128, dtype=jnp.int32)
    wide, narrow = peer_of(steps, 1)
    expert_at = wide * 8 + narrow
    named = expert_ids[:, :, None] == expert_at[None, None, :]
    chosen = jnp.any(named, axis=1)
    share = jnp.sum(jnp.where(named, gate_weights[:, :, None], 0.0), axis=1)
    before = iota2((128, 128), 0) > iota2((128, 128), 1)
    rank = jnp.where(chosen, dot(before.astype(BF), chosen.astype(BF)), -1.0)
    share_hi = share.astype(BF)
    share_lo = (share - share_hi.astype(F32)).astype(BF)

    vmem = pl.BlockSpec(memory_space=pltpu.VMEM)
    hbm = pl.BlockSpec(memory_space=pl.ANY)
    return pl.pallas_call(
        block_kernel,
        out_shape=jax.ShapeDtypeStruct((128, 4096), BF),
        in_specs=[hbm] * 4 + [vmem] * 5 + [hbm] * 3,
        out_specs=vmem,
        scratch_shapes=[
            pltpu.VMEM((2048, 2304), BF),
            pltpu.VMEM((2048, 2304), BF),
            pltpu.VMEM((2048, 2304), BF),
            pltpu.VMEM((4096, 768), BF),
            pltpu.VMEM((4096, 768), BF),
            pltpu.VMEM((768, 4096), BF),
            pltpu.VMEM((256, 2048), BF),
            pltpu.VMEM((128, 4096), BF),
            pltpu.VMEM((288, 4096), BF),
            pltpu.VMEM((288, 768), BF),
            pltpu.VMEM((256, 2048), F32),
            pltpu.VMEM((8, 512, 128), BF),
            pltpu.VMEM((2, 1024, 128), BF),
            pltpu.VMEM((256, 512), BF),
            pltpu.SemaphoreType.REGULAR,
            pltpu.SemaphoreType.DMA((6,)),
            pltpu.SemaphoreType.DMA((8,)),
            pltpu.SemaphoreType.DMA((8,)),
            pltpu.SemaphoreType.DMA((8,)),
            pltpu.SemaphoreType.DMA((8,)),
            pltpu.SemaphoreType.DMA((4,)),
            pltpu.SemaphoreType.DMA((4,)),
            pltpu.SemaphoreType.DMA((2,)),
            pltpu.SemaphoreType.DMA((2,)),
            pltpu.SemaphoreType.DMA((2,)),
            pltpu.SemaphoreType.DMA((2,)),
            pltpu.SemaphoreType.DMA((128,)),
            pltpu.SemaphoreType.DMA((128,)),
            pltpu.SemaphoreType.DMA((128,)),
            pltpu.SemaphoreType.DMA((128,)),
        ],
        compiler_params=pltpu.CompilerParams(
            collective_id=1, has_side_effects=True, vmem_limit_bytes=62 * 2**20
        ),
        cost_estimate=pl.CostEstimate(
            flops=32_000_000_000, bytes_accessed=30_000_000, transcendentals=5_000_000
        ),
    )(
        q_in,
        kv_in,
        residual,
        out_proj,
        norm_gain.reshape(1, 4096),
        rank,
        rank.T,
        share_hi,
        share_lo,
        w_gate,
        w_up,
        w_down,
    )


def solution(mesh):
    in_specs = (
        P(("wide", "narrow"), None, None),
        P(("wide", "narrow"), None, None),
        P(("wide", "narrow"), None, None),
        P(("wide", "narrow"), None),
        P("narrow", None),
        P(),
        P(("wide", "narrow"), None),
        P(("wide", "narrow"), None),
        P(("wide", "narrow"), None, None),
        P(("wide", "narrow"), None, None),
        P(("wide", "narrow"), None, None),
    )
    out_specs = P(("wide", "narrow"), None)
    return jax.shard_map(shards, mesh=mesh, in_specs=in_specs, out_specs=out_specs, check_vma=False)
```

time: 416 us -> 319 us (0.77); the launches traced: 416 us -> 314 us
  waiting for transfers between devices: 57.9 us -> 0 us
  Pallas kernels: 272 us -> 303 us
  matrix products: 20.6 us -> 0.21 us
  starting transfers between devices: 15.4 us -> 0 us
  between operations: 13.7 us -> 0.04 us
  local copies, waits for them, and re-layouts: 21.1 us -> 8.29 us
  other arithmetic: 14.8 us -> 1.99 us
    reduce_scatter x1 -> x0, waiting for transfers between devices: 41.5 us -> none  [shards(): lax.psum_scatter(jnp.dot(attended, out_proj, preferred_element_type=jnp.f...]
    pallas_call x1, Pallas kernels: 272 us -> 303 us  [shards(): pl.pallas_call(block_kernel, out_shape=jax.ShapeDtypeStruct((128, 4096),...]
    dot_general x4 -> x1, matrix products: 20.6 us -> 0.21 us  [dot(): return jnp.dot(a, b, preferred_element_type=F32)]
    all_to_all x3 -> x0, waiting for transfers between devices: 16.4 us -> none  [the longest x1 12.4 us: shards(): lax.all_to_all(queries, 'narrow', split_axis=1, concat_axis=0, tiled=True)]
    all_to_all x3 -> x0, starting transfers between devices: 15.4 us -> none  [the longest x1 6.81 us: shards(): lax.all_to_all(queries, 'narrow', split_axis=1, concat_axis=0, tiled=True)]
    unnamed x30 -> x5, local copies, waits for them, and re-layouts: 11.5 us -> 3.87 us
  transfers between devices with their start and end apart: 4 -> 0, of which waited for: 3 -> 0; matrix products, arithmetic and copies ran while one was open for 6% -> 0% of each run, Pallas kernels for 0% -> 0%
where the time goes in v4:
time: 319 us; the launch traced here: 314 us
  Pallas kernels  303 us (95%)
  local copies, waits for them, and re-layouts  8.29 us (3%)
    pallas_call x1, Pallas kernels, shards(): pl.pallas_call(block_kernel, out_shape=jax.ShapeDtypeStruct((128, 4096),...  303 us

profile of v4, /device:TPU:1, one launch (start us, length us, event | category | flops | bytes accessed | tf_op | source)
XLA Modules:
  0.0 313.6 jit_solution(15261780684048382750)
XLA Ops:
  0.0 0.8 copy.22
  0.8 0.3 compare_reduce_fusion
  1.1 0.1 copy.23
  1.2 0.2 convolution_select_fusion
  1.4 0.0 copy-start
  1.4 0.7 copy.26.rank
  2.1 0.8 copy.25
  2.9 0.3 fusion
  3.2 0.6 subtract_convert_fusion
  3.9 1.0 copy_bitcast_fusion
  4.9 0.7 maximum_bitcast_fusion.kv_in
  5.6 2.6 copy.19
  8.2 0.0 copy-done
  8.2 303.1 %shard_map.109 = bf16[128,4096]{1,0:T(8,128)(2,1)} custom-call(bf16[8,512,128]{2,1,0:T(8,128)(2,1)} %bitcast.12, bf16[4,2,128,128]{3,2,1,0:T(8,128)(2,1)} %maximum_bitcast_fusion.kv_in, bf16[128,4096]{1,0:T(8,128)(2,1)} %res_hbm.1, bf16[512,4096]{1,0:T(8,128)(2,1)} %proj_hbm.1, f32[1,4096]{1,0:T(1,128)} %bitcast.14, f32[128,128]{1,0:T(8,128)} %copy.26.rank, ...), custom_call_target="tpu_custom_call" | custom-call | flops 32000000000 | bytes 30000000 | tf_op jit(solution)/shard_map/pallas_call | solution.py:524
  311.3 2.3 copy.32
  (1 shorter events, 0.0 us)
Async XLA Ops:
  1.4 6.8 %copy-start = (f32[128,128]{0,1:T(8,128)}, f32[128,128]{0,1:T(8,128)S(1)}, u32[]{:S(2)}) copy-start(f32[128,128]{0,1:T(8,128)S(1)} %convolution_select_fusion) | copy-start | bytes 196612

commit v5 on v4

--- a/solution.py
+++ b/solution.py
@@ -41,10 +41,8 @@
     res_hbm,
     proj_hbm,
     gain,
-    rank,
-    rank_t,
-    share_hi,
-    share_lo,
+    ids,
+    gates,
     wg_hbm,
     wu_hbm,
     wd_hbm,
@@ -63,6 +61,10 @@
     q_all,
     kv_all,
     mixed,
+    rank,
+    rank_t,
+    share_hi,
+    share_lo,
     row_in,
     w_sem,
     q_send,
@@ -142,7 +144,7 @@
     pl.semaphore_wait(barrier, 22)
     for s in (4, 5, 2, 6, 3, 7, 1):
         send_kv(s).start()
-    for s in (4, 5, 2, 6, 3, 7, 1):
+    for s in (4, 5, 1):
         send_q(s).start()
     for d in range(1, 8):
         pl.semaphore_signal(row_in, inc=1, device_id=(wide, (narrow + d) & 7), device_id_type=MESH)
@@ -182,9 +184,30 @@
             folded_at(stage, 1 + i), folded_at(ret, 4 + i), l_send, l_recv, i, at((1, 3)[i], 0)
         )
 
+    wide_at, narrow_at = peer_of(iota2((128, 128), 1), 1)
+    expert_at = wide_at * 8 + narrow_at
+    chosen = jnp.zeros((128, 128), F32)
+    share = jnp.zeros((128, 128), F32)
+    for i in range(8):
+        named = ids[:, i : i + 1] == expert_at
+        chosen = jnp.where(named, 1.0, chosen)
+        share = jnp.where(named, gates[:, i : i + 1], share)
+    tri_row, tri_col = iota2((128, 128), 0), iota2((128, 128), 1)
+    before = jnp.where(tri_row > tri_col, 1.0, 0.0).astype(BF)
+    same = jnp.where(tri_row == tri_col, 1.0, 0.0).astype(BF)
+    ranked = jnp.where(chosen > 0.5, dot(before, chosen.astype(BF)), -1.0)
+    rank[...] = ranked
+    rank_t[...] = lax.dot_general(
+        same, ranked.astype(BF), (((1,), (1,)), ((), ())), preferred_element_type=F32
+    )
+    share_hi[...] = share.astype(BF)
+    share_lo[...] = (share - share.astype(BF).astype(F32)).astype(BF)
+
     own_kv.wait()
     for s in range(1, 8):
         send_kv(s).wait_recv()
+    for s in (6, 7, 2, 3):
+        send_q(s).start()
     load_proj.wait()
 
     scale = math.log2(math.e) / math.sqrt(128)
@@ -508,23 +531,12 @@
 ):
     q_in = jnp.transpose(queries, (1, 0, 2)).reshape(8, 512, 128)
     kv_in = jnp.transpose(jnp.stack([keys, values]), (2, 0, 1, 3))
-    steps = jnp.arange(128, dtype=jnp.int32)
-    wide, narrow = peer_of(steps, 1)
-    expert_at = wide * 8 + narrow
-    named = expert_ids[:, :, None] == expert_at[None, None, :]
-    chosen = jnp.any(named, axis=1)
-    share = jnp.sum(jnp.where(named, gate_weights[:, :, None], 0.0), axis=1)
-    before = iota2((128, 128), 0) > iota2((128, 128), 1)
-    rank = jnp.where(chosen, dot(before.astype(BF), chosen.astype(BF)), -1.0)
-    share_hi = share.astype(BF)
-    share_lo = (share - share_hi.astype(F32)).astype(BF)
-
     vmem = pl.BlockSpec(memory_space=pltpu.VMEM)
     hbm = pl.BlockSpec(memory_space=pl.ANY)
     return pl.pallas_call(
         block_kernel,
         out_shape=jax.ShapeDtypeStruct((128, 4096), BF),
-        in_specs=[hbm] * 4 + [vmem] * 5 + [hbm] * 3,
+        in_specs=[hbm] * 4 + [vmem] * 3 + [hbm] * 3,
         out_specs=vmem,
         scratch_shapes=[
             pltpu.VMEM((2048, 2304), BF),
@@ -541,6 +553,10 @@
             pltpu.VMEM((8, 512, 128), BF),
             pltpu.VMEM((2, 1024, 128), BF),
             pltpu.VMEM((256, 512), BF),
+            pltpu.VMEM((128, 128), F32),
+            pltpu.VMEM((128, 128), F32),
+            pltpu.VMEM((128, 128), BF),
+            pltpu.VMEM((128, 128), BF),
             pltpu.SemaphoreType.REGULAR,
             pltpu.SemaphoreType.DMA((6,)),
             pltpu.SemaphoreType.DMA((8,)),
@@ -570,10 +586,8 @@
         residual,
         out_proj,
         norm_gain.reshape(1, 4096),
-        rank,
-        rank.T,
-        share_hi,
-        share_lo,
+        expert_ids,
+        gate_weights,
         w_gate,
         w_up,
         w_down,

time: 319 us -> 321 us (level)
  Pallas kernels: 303 us -> 307 us
    pallas_call x1, Pallas kernels: 303 us -> 307 us  [shards(): pl.pallas_call(block_kernel, out_shape=jax.ShapeDtypeStruct((128, 4096),...]
where the time goes in v5:
time: 321 us; the launch traced here: 317 us
  Pallas kernels  307 us (96%)
  local copies, waits for them, and re-layouts  8.7 us (3%)
    pallas_call x1, Pallas kernels, shards(): pl.pallas_call(block_kernel, out_shape=jax.ShapeDtypeStruct((128, 4096),...  307 us

profile of v5, /device:TPU:1, one launch (start us, length us, event | category | flops | bytes accessed | tf_op | source)
XLA Modules:
  0.0 316.8 jit_solution(17646101932440116700)
XLA Ops:
  0.0 1.4 copy.15.ids
  1.4 1.4 copy.16.gates
  2.8 1.0 copy_bitcast_fusion
  3.8 0.7 maximum_bitcast_fusion.kv_in
  4.6 2.6 copy.12
  7.2 307.3 %shard_map.109 = bf16[128,4096]{1,0:T(8,128)(2,1)} custom-call(bf16[8,512,128]{2,1,0:T(8,128)(2,1)} %bitcast.10, bf16[4,2,128,128]{3,2,1,0:T(8,128)(2,1)} %maximum_bitcast_fusion.kv_in, bf16[128,4096]{1,0:T(8,128)(2,1)} %res_hbm.1, bf16[512,4096]{1,0:T(8,128)(2,1)} %proj_hbm.1, f32[1,4096]{1,0:T(1,128)} %bitcast.11, s32[128,8]{1,0:T(8,128)} %copy.15.ids, ...), custom_call_target="tpu_custom_call" | custom-call | flops 32000000000 | bytes 30000000 | tf_op jit(solution)/shard_map/pallas_call | solution.py:536
  314.5 2.3 copy.20

commit v6 on v5

--- a/solution.py
+++ b/solution.py
@@ -144,7 +144,7 @@
     pl.semaphore_wait(barrier, 22)
     for s in (4, 5, 2, 6, 3, 7, 1):
         send_kv(s).start()
-    for s in (4, 5, 1):
+    for s in (4, 5, 2, 6, 3, 7, 1):
         send_q(s).start()
     for d in range(1, 8):
         pl.semaphore_signal(row_in, inc=1, device_id=(wide, (narrow + d) & 7), device_id_type=MESH)
@@ -184,30 +184,30 @@
             folded_at(stage, 1 + i), folded_at(ret, 4 + i), l_send, l_recv, i, at((1, 3)[i], 0)
         )
 
-    wide_at, narrow_at = peer_of(iota2((128, 128), 1), 1)
+    wide_at, narrow_at = peer_of(iota2((128, 128), 0), 1)
     expert_at = wide_at * 8 + narrow_at
     chosen = jnp.zeros((128, 128), F32)
     share = jnp.zeros((128, 128), F32)
     for i in range(8):
-        named = ids[:, i : i + 1] == expert_at
+        named = ids[i : i + 1, :] == expert_at
         chosen = jnp.where(named, 1.0, chosen)
-        share = jnp.where(named, gates[:, i : i + 1], share)
+        share = jnp.where(named, gates[i : i + 1, :], share)
     tri_row, tri_col = iota2((128, 128), 0), iota2((128, 128), 1)
-    before = jnp.where(tri_row > tri_col, 1.0, 0.0).astype(BF)
+    before = jnp.where(tri_row < tri_col, 1.0, 0.0).astype(BF)
     same = jnp.where(tri_row == tri_col, 1.0, 0.0).astype(BF)
-    ranked = jnp.where(chosen > 0.5, dot(before, chosen.astype(BF)), -1.0)
-    rank[...] = ranked
-    rank_t[...] = lax.dot_general(
-        same, ranked.astype(BF), (((1,), (1,)), ((), ())), preferred_element_type=F32
-    )
-    share_hi[...] = share.astype(BF)
-    share_lo[...] = (share - share.astype(BF).astype(F32)).astype(BF)
+
+    def turned(a):
+        return lax.dot_general(same, a, (((1,), (1,)), ((), ())), preferred_element_type=F32)
+
+    ranked = jnp.where(chosen > 0.5, dot(chosen.astype(BF), before), -1.0)
+    rank_t[...] = ranked
+    rank[...] = turned(ranked.astype(BF))
+    share_hi[...] = turned(share.astype(BF)).astype(BF)
+    share_lo[...] = turned((share - share.astype(BF).astype(F32)).astype(BF)).astype(BF)
 
     own_kv.wait()
     for s in range(1, 8):
         send_kv(s).wait_recv()
-    for s in (6, 7, 2, 3):
-        send_q(s).start()
     load_proj.wait()
 
     scale = math.log2(math.e) / math.sqrt(128)
@@ -586,8 +586,8 @@
         residual,
         out_proj,
         norm_gain.reshape(1, 4096),
-        expert_ids,
-        gate_weights,
+        expert_ids.T,
+        gate_weights.T,
         w_gate,
         w_up,
         w_down,

time: 321 us -> 314 us (0.978)
  the two profiles are of different devices: /device:TPU:1 before, /device:TPU:24 now
where the time goes in v6:
time: 314 us
  Pallas kernels  307 us (98%)
  local copies, waits for them, and re-layouts  5.89 us (2%)
    pallas_call x1, Pallas kernels, shards(): pl.pallas_call(block_kernel, out_shape=jax.ShapeDtypeStruct((128, 4096),...  307 us

profile of v6, /device:TPU:24, one launch (start us, length us, event | category | flops | bytes accessed | tf_op | source)
XLA Modules:
  0.0 313.6 jit_solution(12863516016671958996)
XLA Ops:
  0.0 1.0 copy_bitcast_fusion
  1.0 0.7 maximum_bitcast_fusion.kv_in
  1.7 2.6 copy.12
  4.3 306.9 %shard_map.109 = bf16[128,4096]{1,0:T(8,128)(2,1)} custom-call(bf16[8,512,128]{2,1,0:T(8,128)(2,1)} %bitcast.12, bf16[4,2,128,128]{3,2,1,0:T(8,128)(2,1)} %maximum_bitcast_fusion.kv_in, bf16[128,4096]{1,0:T(8,128)(2,1)} %res_hbm.1, bf16[512,4096]{1,0:T(8,128)(2,1)} %proj_hbm.1, f32[1,4096]{1,0:T(1,128)} %bitcast.13, s32[8,128]{1,0:T(8,128)} %bitcast.14, ...), custom_call_target="tpu_custom_call" | custom-call | flops 32000000000 | bytes 30000000 | tf_op jit(solution)/shard_map/pallas_call | solution.py:536
  311.3 2.3 copy.18

commit v7 on v6

--- a/solution.py
+++ b/solution.py
@@ -14,7 +14,7 @@
 
 def offset_of(k):
     j = (128 - k) & 127
-    return j, (j >> 2) + j, (j >> 4) + (j >> 2) + j, j >> 6
+    return j, (j >> 2) + 2 * j, (j >> 4) + (j >> 2) + j, j >> 6
 
 
 def peer_of(k, sign):

time: 314 us -> 311 us (level)
  the two profiles are of different devices: /device:TPU:24 before, /device:TPU:1 now
where the time goes in v7:
time: 311 us
  Pallas kernels  305 us (98%)
  local copies, waits for them, and re-layouts  5.89 us (2%)
    pallas_call x1, Pallas kernels, shards(): pl.pallas_call(block_kernel, out_shape=jax.ShapeDtypeStruct((128, 4096),...  305 us

profile of v7, /device:TPU:1, one launch (start us, length us, event | category | flops | bytes accessed | tf_op | source)
XLA Modules:
  0.0 311.2 jit_solution(3331297746305619056)
XLA Ops:
  0.0 1.0 copy_bitcast_fusion
  1.0 0.7 maximum_bitcast_fusion.kv_in
  1.7 2.6 copy.12
  4.3 304.6 %shard_map.109 = bf16[128,4096]{1,0:T(8,128)(2,1)} custom-call(bf16[8,512,128]{2,1,0:T(8,128)(2,1)} %bitcast.12, bf16[4,2,128,128]{3,2,1,0:T(8,128)(2,1)} %maximum_bitcast_fusion.kv_in, bf16[128,4096]{1,0:T(8,128)(2,1)} %res_hbm.1, bf16[512,4096]{1,0:T(8,128)(2,1)} %proj_hbm.1, f32[1,4096]{1,0:T(1,128)} %bitcast.13, s32[8,128]{1,0:T(8,128)} %bitcast.14, ...), custom_call_target="tpu_custom_call" | custom-call | flops 32000000000 | bytes 30000000 | tf_op jit(solution)/shard_map/pallas_call | solution.py:536
  309.0 2.3 copy.18
